TPU v7x, 32 devices: a whole 2x2x4 slice. The times are simulated.
32 devices in a mesh: groups: 2 (over y), img: 4 (over z), pair: 4 (over x, core).
Axes of the slice: x: 2, y: 2, z: 4, core: 2. Of those that a mesh axis runs over, the one named last changes fastest.
Arguments:
- pair_images: int32 [128, 2], P(('groups', 'img')), parts along dimension 0, may hold values from 0 to 31, as said below
- pointmaps: bfloat16 [128, 2, 3, 50176], P(('groups', 'img'), None, None, 'pair'), parts along dimension 0, may hold values from -6 to 6
- confidence: bfloat16 [128, 2, 50176], P(('groups', 'img'), None, 'pair'), parts along dimension 0, may hold values from 1 to 10
- log_depth: float32 [64, 50176], P(('groups', 'img'), 'pair'), parts along dimension 0, may hold values from -0.5 to 0.5
- image_params: float32 [64, 7], P(('groups', 'img')), parts along dimension 0, may hold values from -0.3 to 0.3
- pair_params: float32 [128, 7], P(('groups', 'img')), parts along dimension 0, may hold values from -0.3 to 0.3
Outputs:
- new_depth: float32 [64, 50176], P(('groups', 'img'), 'pair'), parts along dimension 0
- new_images: float32 [64, 7], P(('groups', 'img')), parts along dimension 0
- new_pairs: float32 [128, 7], P(('groups', 'img')), parts along dimension 0
There are 2 independent parts, one for each index of `groups`. A program takes and returns all parts, laid end to end along the dimension named above; each array names one. Nothing has to cross between parts.
Inputs may be any that keep to these rules, and one draw needn't show every extreme that they name: pair_images[e, 0] is one of the 8 images of block e // 16, i.e. between (e // 16) * 8 and that plus 8 - 1; the two images of a pair differ; within each aligned block of 16 pairs at most 8 second images lie in any one aligned block of 8 images, and exactly 8 in some block.
All inputs are finite; a program needn't handle non-finite values.
Results may differ from a plain program's by a relative error of at most 0.0003.
Values may be sent and summed in bfloat16 or wider, within the bound.
A program may use at most 128 MiB of HBM per device.

v0:
```python
import jax
import jax.numpy as jnp
from jax import lax
from jax.sharding import PartitionSpec as P

SIDE = 224
STEPS = 3


def rotate(w, v):
    scale = 2.0 / (1.0 + w[0] * w[0] + w[1] * w[1] + w[2] * w[2])
    c0 = w[1] * v[2] - w[2] * v[1]
    c1 = w[2] * v[0] - w[0] * v[2]
    c2 = w[0] * v[1] - w[1] * v[0]
    e0 = w[1] * c2 - w[2] * c1
    e1 = w[2] * c0 - w[0] * c2
    e2 = w[0] * c1 - w[1] * c0
    return jnp.stack([v[0] + scale * (c0 + e0), v[1] + scale * (c1 + e1), v[2] + scale * (c2 + e2)])


def rot_matrix(w):
    return rotate(w, jnp.eye(3, dtype=jnp.float32))


def apply_matrix(mat, vec):
    return jnp.stack(
        [mat[row, 0] * vec[0] + mat[row, 1] * vec[1] + mat[row, 2] * vec[2] for row in range(3)]
    )


def apply_transpose(mat, vec):
    return jnp.stack(
        [mat[0, col] * vec[0] + mat[1, col] * vec[1] + mat[2, col] * vec[2] for col in range(3)]
    )


def rotation_grad(w, moment):

    def traced(ww):
        return jnp.sum(rot_matrix(ww) * moment)

    value, pull = jax.vjp(traced, w)
    return pull(jnp.ones_like(value))[0]


def outer_sum(left, right):
    return jnp.einsum(
        "jp,kp->jk",
        left,
        right,
        precision=lax.Precision.HIGHEST,
        preferred_element_type=jnp.float32,
    )


def view_grads(depth, image, pose, maps, conf, coord_a, coord_b):
    points = maps.astype(jnp.float32)
    weight = conf.astype(jnp.float32)
    focal = jnp.exp(image[0])
    dist = jnp.exp(depth)
    camera = jnp.stack([dist * coord_a / focal, dist * coord_b / focal, dist])
    rot_img = rot_matrix(image[1:4])
    rot_pose = rot_matrix(pose[1:4])
    factor = jnp.exp(pose[0])
    turned = apply_matrix(rot_img, camera)
    moved = factor * apply_matrix(rot_pose, points)
    resid = turned + image[4:7][:, None] - moved - pose[4:7][:, None]
    pulled = 2.0 * weight[None, :] * resid
    d_shift = jnp.sum(pulled, 1)
    d_scale = -jnp.sum(pulled * moved)
    back = apply_transpose(rot_img, pulled)
    d_depth = back[0] * camera[0] + back[1] * camera[1] + back[2] * camera[2]
    d_focal = -jnp.sum(back[0] * camera[0] + back[1] * camera[1])
    d_turn = rotation_grad(image[1:4], outer_sum(pulled, camera))
    d_spin = rotation_grad(pose[1:4], -factor * outer_sum(pulled, points))
    d_image = jnp.concatenate([d_focal[None], d_turn, d_shift])
    d_pose = jnp.concatenate([d_scale[None], d_spin, -d_shift])
    curv = (
        2.0
        * weight
        * dist
        * dist
        * ((coord_a * coord_a + coord_b * coord_b) / (focal * focal) + 1.0)
    )
    return (d_depth, d_image, d_pose, curv, jnp.sum(weight))


def many_views(depth, image, pose, maps, conf, coord_a, coord_b):
    mapped = jax.vmap(view_grads, in_axes=(0, 0, 0, 0, 0, None, None))
    return mapped(depth, image, pose, maps, conf, coord_a, coord_b)


def matmul(left, right):
    return jnp.dot(left, right, precision=lax.Precision.HIGHEST, preferred_element_type=jnp.float32)


def per_device(pair_images, pointmaps, confidence, log_depth, image_params, pair_params):
    pair_dev = pair_images.shape[0]
    img_dev = log_depth.shape[0]
    pix_dev = log_depth.shape[1]
    blocks = lax.axis_size("img")
    slots = max(2, 2 * pair_dev // blocks)
    here = lax.axis_index("img")
    pixel = lax.axis_index("pair") * pix_dev + jnp.arange(pix_dev)
    coord_a = ((pixel % SIDE).astype(jnp.float32) - (SIDE - 1) / 2.0) / SIDE
    coord_b = ((pixel // SIDE).astype(jnp.float32) - (SIDE - 1) / 2.0) / SIDE
    rate_img = jnp.array([0.1, 0.02, 0.02, 0.02, 0.3, 0.3, 0.3], jnp.float32)
    rate_pair = jnp.array([0.05, 0.02, 0.02, 0.02, 0.3, 0.3, 0.3], jnp.float32)
    first = pair_images[:, 0] - here * img_dev
    target = pair_images[:, 1] // img_dev
    second_in = pair_images[:, 1] - target * img_dev
    hits = (target[:, None] == jnp.arange(blocks)[None, :]).astype(jnp.int32)
    rank = jnp.sum(jnp.cumsum(hits, 0) * hits, 1) - 1
    place = target * slots + rank
    spread = (place[None, :] == jnp.arange(blocks * slots)[:, None]).astype(jnp.float32)
    wanted = (
        jnp.full((blocks * slots,), -1, jnp.int32).at[place].set(second_in).reshape(blocks, slots)
    )
    asked = lax.all_to_all(wanted, "img", split_axis=0, concat_axis=0, tiled=True).reshape(-1)
    valid = asked >= 0
    pick = jnp.maximum(asked, 0)
    collect = ((pick[None, :] == jnp.arange(img_dev)[:, None]) & valid[None, :]).astype(jnp.float32)
    owned = (first[None, :] == jnp.arange(img_dev)[:, None]).astype(jnp.float32)
    for step in range(STEPS):
        d_z, d_i, d_p, curv, wsum = many_views(
            log_depth[first],
            image_params[first],
            pair_params,
            pointmaps[:, 0],
            confidence[:, 0],
            coord_a,
            coord_b,
        )
        grad_z = matmul(owned, d_z)
        curv_z = matmul(owned, curv)
        grad_i = matmul(owned, d_i)
        weight_i = matmul(owned, wsum[:, None])[:, 0]
        grad_p = d_p
        weight_p = wsum
        got_z, got_i = (
            lax.all_to_all(
                log_depth[pick].reshape(blocks, slots, pix_dev),
                "img",
                split_axis=0,
                concat_axis=0,
                tiled=True,
            ),
            lax.all_to_all(
                image_params[pick].reshape(blocks, slots, 7),
                "img",
                split_axis=0,
                concat_axis=0,
                tiled=True,
            ),
        )
        far_z = got_z.reshape(blocks * slots, pix_dev)[place]
        far_i = got_i.reshape(blocks * slots, 7)[place]
        e_z, e_i, e_p, e_curv, e_sum = many_views(
            far_z, far_i, pair_params, pointmaps[:, 1], confidence[:, 1], coord_a, coord_b
        )
        grad_p = grad_p + e_p
        weight_p = weight_p + e_sum
        back_z = matmul(spread, e_z).reshape(blocks, slots, pix_dev)
        back_curv = matmul(spread, e_curv).reshape(blocks, slots, pix_dev)
        back_small = matmul(spread, jnp.concatenate([e_i, e_sum[:, None]], 1)).reshape(
            blocks, slots, 8
        )
        in_z, in_curv, in_small = (
            lax.all_to_all(back_z, "img", split_axis=0, concat_axis=0, tiled=True),
            lax.all_to_all(back_curv, "img", split_axis=0, concat_axis=0, tiled=True),
            lax.all_to_all(back_small, "img", split_axis=0, concat_axis=0, tiled=True),
        )
        in_small = in_small.reshape(blocks * slots, 8)
        grad_z = grad_z + matmul(collect, in_z.reshape(blocks * slots, pix_dev))
        curv_z = curv_z + matmul(collect, in_curv.reshape(blocks * slots, pix_dev))
        grad_i = grad_i + matmul(collect, in_small[:, :7])
        weight_i = weight_i + matmul(collect, in_small[:, 7:8])[:, 0]
        grad_i, weight_i, grad_p, weight_p = lax.psum((grad_i, weight_i, grad_p, weight_p), "pair")
        log_depth = log_depth - grad_z / (curv_z + 1.0)
        image_params = image_params - rate_img[None, :] * grad_i / (weight_i[:, None] + 1.0)
        pair_params = pair_params - rate_pair[None, :] * grad_p / (weight_p[:, None] + 1.0)
    return (log_depth, image_params, pair_params)


def solution(mesh):
    in_specs = (
        P(("groups", "img"), None),
        P(("groups", "img"), None, None, "pair"),
        P(("groups", "img"), None, "pair"),
        P(("groups", "img"), "pair"),
        P(("groups", "img"), None),
        P(("groups", "img"), None),
    )
    out_specs = (
        P(("groups", "img"), "pair"),
        P(("groups", "img"), None),
        P(("groups", "img"), None),
    )
    return jax.shard_map(
        per_device, mesh=mesh, in_specs=in_specs, out_specs=out_specs, check_vma=False
    )
```

profile of v0, /device:TPU:0, one launch (start us, length us, event | category | flops | bytes accessed | tf_op | source)
XLA Modules:
  0.0 788.4 jit_solution(1235520401865329002)
XLA Ops:
  4.9 6.3 all-to-all-start
  17.2 6.9 fusion.585
  27.8 3.3 fusion.582
  35.7 5.1 all-to-all-start.1
  43.0 3.3 all-to-all-done.1
  46.4 3.8 all-to-all-start.2
  51.9 3.3 multiply_add_fusion.35
  59.7 26.4 %all-to-all-done.2 = f32[4,8,12544]{2,1,0:T(8,128)S(1)} async-done(((f32[4,8,12544]{2,1,0:T(8,128)}), f32[4,8,12544]{2,1,0:T(8,128)S(1)}, u32[]{:S(2)}, u32[]{:S(2)}) %all-to-all-start.2) | async-done | bytes 1605664 | tf_op jit(solution)/shard_map/all_to_all | solution.py:141
  90.1 4.5 multiply_reduce_fusion.4
  96.5 8.0 %fusion.81 = f32[16,3,3]{2,1,0:T(4,128)S(1)} fusion(bf16[16,3,12544]{2,0,1:T(8,128)(2,1)S(1)} %copy-done.60, f32[16,3,12544]{2,0,1:T(8,128)S(1)} %get-tuple-element.508, f32[16]{0:T(128)S(1)} %fusion.558), kind=kOutput, calls=%fused_computation.138 | convolution fusion | flops 21676176 | bytes 3613312 | tf_op jit(solution)/shard_map/vmap(jp,kp->jk)/dot_general | solution.py:47
  104.8 3.7 fusion.172
  108.5 18.2 %fusion.86 = f32[16,3,3]{2,1,0:T(4,128)S(1)} fusion(bf16[16,3,12544]{2,0,1:T(8,128)(2,1)S(1)} %copy-done.57, f32[16,3,12544]{2,0,1:T(8,128)S(1)} %copy-done.8, f32[16]{0:T(128)S(1)} %fusion.558), kind=kOutput, calls=%fused_computation.139 | convolution fusion | flops 21676176 | bytes 3613312 | tf_op jit(solution)/shard_map/vmap(jp,kp->jk)/dot_general | solution.py:47
  128.7 24.0 %fusion.31 = f32[16,3,3]{2,1,0:T(4,128)S(1)} fusion(f32[16,3,12544]{2,0,1:T(8,128)S(1)} %get-tuple-element.508, f32[3,16,12544]{2,1,0:T(8,128)S(1)} %pad_maximum_fusion), kind=kOutput, calls=%fused_computation.56 | convolution fusion | flops 21676032 | bytes 4817472 | tf_op jit(solution)/shard_map/vmap(jp,kp->jk)/dot_general | solution.py:47
  155.4 24.0 %fusion.27 = f32[16,3,3]{2,1,0:T(4,128)S(1)} fusion(f32[16,3,12544]{2,0,1:T(8,128)S(1)} %copy-done.9, f32[3,16,12544]{2,1,0:T(8,128)S(1)} %pad_maximum_fusion.1), kind=kOutput, calls=%fused_computation.52 | convolution fusion | flops 21676032 | bytes 4817472 | tf_op jit(solution)/shard_map/vmap(jp,kp->jk)/dot_general | solution.py:47
  183.8 3.2 all-to-all-start.5
  187.1 4.7 fusion.177
  193.7 2.8 fusion.122
  198.9 6.0 all-reduce.182
  208.8 4.9 all-to-all-start.6
  214.5 4.9 all-to-all-done.6
  219.3 4.4 all-to-all-start.4
  229.9 30.4 %all-to-all-done.4 = f32[4,8,12544]{2,1,0:T(8,128)} async-done(((f32[4,8,12544]{2,1,0:T(8,128)}), f32[4,8,12544]{2,1,0:T(8,128)}, u32[]{:S(2)}, u32[]{:S(2)}) %all-to-all-start.4) | async-done | bytes 1605664 | tf_op jit(solution)/shard_map/all_to_all | solution.py:170
  260.3 4.4 all-to-all-start.3
  264.7 2.3 multiply_add_fusion.15
  269.2 32.7 %all-to-all-done.3 = f32[4,8,12544]{2,1,0:T(8,128)} async-done(((f32[4,8,12544]{2,1,0:T(8,128)}), f32[4,8,12544]{2,1,0:T(8,128)}, u32[]{:S(2)}, u32[]{:S(2)}) %all-to-all-start.3) | async-done | bytes 1605664 | tf_op jit(solution)/shard_map/all_to_all | solution.py:169
  307.0 3.7 all-to-all-start.7
  314.3 33.5 %all-to-all-done.7 = f32[4,8,12544]{2,1,0:T(8,128)S(1)} async-done(((f32[4,8,12544]{2,1,0:T(8,128)}), f32[4,8,12544]{2,1,0:T(8,128)S(1)}, u32[]{:S(2)}, u32[]{:S(2)}) %all-to-all-start.7) | async-done | bytes 1605664 | tf_op jit(solution)/shard_map/all_to_all | solution.py:141
  351.9 5.2 multiply_reduce_fusion.2
  357.2 2.4 fusion.571
  359.6 8.0 %fusion.91 = f32[16,3,3]{2,1,0:T(4,128)S(1)} fusion(bf16[16,3,12544]{2,0,1:T(8,128)(2,1)S(1)} %copy-done.61, f32[16,3,12544]{2,0,1:T(8,128)S(1)} %get-tuple-element.486, f32[16]{0:T(128)S(1)} %copy-done.251), kind=kOutput, calls=%fused_computation.140 | convolution fusion | flops 21676176 | bytes 3613312 | tf_op jit(solution)/shard_map/vmap(jp,kp->jk)/dot_general | solution.py:47
  367.6 8.2 %fusion.96 = f32[16,3,3]{2,1,0:T(4,128)S(1)} fusion(bf16[16,3,12544]{2,0,1:T(8,128)(2,1)S(1)} %copy-done.58, f32[16,3,12544]{2,0,1:T(8,128)S(1)} %get-tuple-element.485, f32[16]{0:T(128)S(1)} %copy-done.251), kind=kOutput, calls=%fused_computation.141 | convolution fusion | flops 21676176 | bytes 3613312 | tf_op jit(solution)/shard_map/vmap(jp,kp->jk)/dot_general | solution.py:47
  378.0 2.7 fusion.158
  382.9 24.0 %fusion.23 = f32[16,3,3]{2,1,0:T(4,128)S(1)} fusion(f32[16,3,12544]{2,0,1:T(8,128)S(1)} %get-tuple-element.486, f32[3,16,12544]{2,1,0:T(8,128)S(1)} %pad_maximum_fusion.2), kind=kOutput, calls=%fused_computation.48 | convolution fusion | flops 21676032 | bytes 4817472 | tf_op jit(solution)/shard_map/vmap(jp,kp->jk)/dot_general | solution.py:47
  409.6 23.9 %fusion.19 = f32[16,3,3]{2,1,0:T(4,128)S(1)} fusion(f32[16,3,12544]{2,0,1:T(8,128)S(1)} %copy-done.11, f32[3,16,12544]{2,1,0:T(8,128)S(1)} %pad_maximum_fusion.3), kind=kOutput, calls=%fused_computation.44 | convolution fusion | flops 21676032 | bytes 4817472 | tf_op jit(solution)/shard_map/vmap(jp,kp->jk)/dot_general | solution.py:47
  442.0 3.2 all-to-all-start.10
  446.7 2.8 fusion.226
  449.9 2.8 fusion.125
  456.3 6.0 all-reduce.181
  466.2 5.0 all-to-all-start.11
  471.8 5.0 all-to-all-done.11
  476.8 4.4 all-to-all-start.9
  488.0 29.8 %all-to-all-done.9 = f32[4,8,12544]{2,1,0:T(8,128)} async-done(((f32[4,8,12544]{2,1,0:T(8,128)}), f32[4,8,12544]{2,1,0:T(8,128)}, u32[]{:S(2)}, u32[]{:S(2)}) %all-to-all-start.9) | async-done | bytes 1605664 | tf_op jit(solution)/shard_map/all_to_all | solution.py:170
  517.8 4.4 all-to-all-start.8
  522.2 2.4 multiply_add_fusion.2
  526.7 32.6 %all-to-all-done.8 = f32[4,8,12544]{2,1,0:T(8,128)} async-done(((f32[4,8,12544]{2,1,0:T(8,128)}), f32[4,8,12544]{2,1,0:T(8,128)}, u32[]{:S(2)}, u32[]{:S(2)}) %all-to-all-start.8) | async-done | bytes 1605664 | tf_op jit(solution)/shard_map/all_to_all | solution.py:169
  564.5 3.7 all-to-all-start.12
  570.3 34.9 %all-to-all-done.12 = f32[4,8,12544]{2,1,0:T(8,128)S(1)} async-done(((f32[4,8,12544]{2,1,0:T(8,128)}), f32[4,8,12544]{2,1,0:T(8,128)S(1)}, u32[]{:S(2)}, u32[]{:S(2)}) %all-to-all-start.12) | async-done | bytes 1605664 | tf_op jit(solution)/shard_map/all_to_all | solution.py:141
  609.3 5.1 multiply_reduce_fusion
  614.5 2.4 fusion.564
  616.9 8.0 %fusion.101 = f32[16,3,3]{2,1,0:T(4,128)S(1)} fusion(bf16[16,3,12544]{2,0,1:T(8,128)(2,1)S(1)} %copy-done.62, f32[16,3,12544]{2,0,1:T(8,128)S(1)} %get-tuple-element.468, f32[16]{0:T(128)S(1)} %copy-done.250), kind=kOutput, calls=%fused_computation.142 | convolution fusion | flops 21676176 | bytes 3613312 | tf_op jit(solution)/shard_map/vmap(jp,kp->jk)/dot_general | solution.py:47
  624.9 8.2 %fusion.106 = f32[16,3,3]{2,1,0:T(4,128)S(1)} fusion(bf16[16,3,12544]{2,0,1:T(8,128)(2,1)S(1)} %copy-done.59, f32[16,3,12544]{2,0,1:T(8,128)S(1)} %get-tuple-element.467, f32[16]{0:T(128)S(1)} %copy-done.250), kind=kOutput, calls=%fused_computation.143 | convolution fusion | flops 21676176 | bytes 3613312 | tf_op jit(solution)/shard_map/vmap(jp,kp->jk)/dot_general | solution.py:47
  637.6 24.0 %fusion.15 = f32[16,3,3]{2,1,0:T(4,128)S(1)} fusion(f32[16,3,12544]{2,0,1:T(8,128)S(1)} %get-tuple-element.468, f32[3,16,12544]{2,1,0:T(8,128)S(1)} %pad_maximum_fusion.4), kind=kOutput, calls=%fused_computation.40 | convolution fusion | flops 21676032 | bytes 4817472 | tf_op jit(solution)/shard_map/vmap(jp,kp->jk)/dot_general | solution.py:47
  664.3 23.9 %fusion.11 = f32[16,3,3]{2,1,0:T(4,128)S(1)} fusion(f32[16,3,12544]{2,0,1:T(8,128)S(1)} %copy-done.7, f32[3,16,12544]{2,1,0:T(8,128)S(1)} %pad_maximum_fusion.5), kind=kOutput, calls=%fused_computation.36 | convolution fusion | flops 21676032 | bytes 4817472 | tf_op jit(solution)/shard_map/vmap(jp,kp->jk)/dot_general | solution.py:47
  694.2 3.3 all-to-all-start.15
  697.5 3.3 fusion.128
  700.8 2.3 all-to-all-done.15
  703.1 4.4 all-to-all-start.14
  707.9 2.6 fusion.261
  710.9 4.3 fusion.139
  715.4 28.1 %all-to-all-done.14 = f32[4,8,12544]{2,1,0:T(8,128)} async-done(((f32[4,8,12544]{2,1,0:T(8,128)}), f32[4,8,12544]{2,1,0:T(8,128)}, u32[]{:S(2)}, u32[]{:S(2)}) %all-to-all-start.14) | async-done | bytes 1605664 | tf_op jit(solution)/shard_map/all_to_all | solution.py:170
  743.5 4.4 all-to-all-start.13
  750.8 6.3 all-reduce.180
  760.6 24.6 %all-to-all-done.13 = f32[4,8,12544]{2,1,0:T(8,128)} async-done(((f32[4,8,12544]{2,1,0:T(8,128)}), f32[4,8,12544]{2,1,0:T(8,128)}, u32[]{:S(2)}, u32[]{:S(2)}) %all-to-all-start.13) | async-done | bytes 1605664 | tf_op jit(solution)/shard_map/all_to_all | solution.py:169
  785.1 2.8 fusion.7
  (804 shorter events, 135.7 us)
Async XLA Ops:
  0.6 15.8 %copy-start = (f32[8,12544]{1,0:T(8,128)S(1)}, f32[8,12544]{1,0:T(8,128)}, u32[]{:S(2)}) copy-start(f32[8,12544]{1,0:T(8,128)} %param.11) | copy-start | bytes 1204228
  4.9 29.5 %all-to-all-start = ((s32[4,1,8]{2,1,0:T(1,128)}), s32[4,1,8]{2,1,0:T(1,128)S(1)}, u32[]{:S(2)}, u32[]{:S(2)}) async-start(s32[4,1,8]{2,1,0:T(1,128)} %bitcast.47), calls=%async_computation | async-start | bytes 4096 | tf_op jit(solution)/shard_map/all_to_all | solution.py:119
  17.2 38.0 %copy-start.18 = (f32[16,12544]{1,0:T(8,128)}, f32[16,12544]{1,0:T(8,128)S(1)}, u32[]{:S(2)}) copy-start(f32[16,12544]{1,0:T(8,128)S(1)} %gather_fusion.1) | copy-start | bytes 2408452
  35.7 10.7 %all-to-all-start.1 = ((f32[4,8,7]{2,1,0:T(8,128)}), f32[4,8,7]{2,1,0:T(8,128)S(1)}, u32[]{:S(2)}, u32[]{:S(2)}) async-start(f32[4,8,7]{2,1,0:T(8,128)} %bitcast.48), calls=%async_computation.1 | async-start | bytes 32768 | tf_op jit(solution)/shard_map/all_to_all | solution.py:148
  46.4 39.7 %all-to-all-start.2 = ((f32[4,8,12544]{2,1,0:T(8,128)}), f32[4,8,12544]{2,1,0:T(8,128)S(1)}, u32[]{:S(2)}, u32[]{:S(2)}) async-start(f32[4,8,12544]{2,1,0:T(8,128)} %bitcast.1783), calls=%async_computation.2 | async-start | bytes 3211264 | tf_op jit(solution)/shard_map/all_to_all | solution.py:141
  155.4 27.5 %copy-start.243 = (f32[16]{0:T(128)S(1)}, f32[16]{0:T(128)}, u32[]{:S(2)}) copy-start(f32[16]{0:T(128)} %copy-done.242) | copy-start | bytes 196
  155.4 27.5 %copy-start.246 = (s32[16]{0:T(128)S(1)}, s32[16]{0:T(128)}, u32[]{:S(2)}) copy-start(s32[16]{0:T(128)} %get-tuple-element.519) | copy-start | bytes 196
  155.4 31.6 %copy-start.236 = (f32[16,1]{0,1:T(1,128)S(1)}, f32[16,1]{0,1:T(1,128)}, u32[]{:S(2)}) copy-start(f32[16,1]{0,1:T(1,128)} %get-tuple-element.518) | copy-start | bytes 196
  155.4 31.7 %copy-start.237 = (s32[4,8]{1,0:T(4,128)S(1)}, s32[4,8]{1,0:T(4,128)}, u32[]{:S(2)}) copy-start(s32[4,8]{1,0:T(4,128)} %multiply_add_fusion.97) | copy-start | bytes 388
  183.8 14.1 %all-to-all-start.5 = ((f32[4,8,8]{1,2,0:T(8,128)}), f32[4,8,8]{1,2,0:T(8,128)S(1)}, u32[]{:S(2)}, u32[]{:S(2)}) async-start(f32[4,8,8]{1,2,0:T(8,128)} %copy.1173), calls=%async_computation.5 | async-start | bytes 32768 | tf_op jit(solution)/shard_map/all_to_all | solution.py:171
  196.5 31.7 %copy-start.4 = (f32[16,3,12544]{2,0,1:T(8,128)S(1)}, f32[16,3,12544]{2,0,1:T(8,128)}, u32[]{:S(2)}) copy-start(f32[16,3,12544]{2,0,1:T(8,128)} %get-tuple-element.876) | copy-start | bytes 7225348
  206.8 19.0 %copy-start.113 = (f32[16]{0:T(128)}, f32[16]{0:T(128)S(1)}, u32[]{:S(2)}) copy-start(f32[16]{0:T(128)S(1)} %broadcast_add_fusion) | copy-start | bytes 196
  208.8 10.5 %all-to-all-start.6 = ((f32[4,8,7]{2,1,0:T(8,128)}), f32[4,8,7]{2,1,0:T(8,128)S(1)}, u32[]{:S(2)}, u32[]{:S(2)}) async-start(f32[4,8,7]{2,1,0:T(8,128)} %bitcast.189), calls=%async_computation.6 | async-start | bytes 32768 | tf_op jit(solution)/shard_map/all_to_all | solution.py:148
  219.3 40.9 %all-to-all-start.4 = ((f32[4,8,12544]{2,1,0:T(8,128)}), f32[4,8,12544]{2,1,0:T(8,128)}, u32[]{:S(2)}, u32[]{:S(2)}) async-start(f32[4,8,12544]{2,1,0:T(8,128)} %fusion.122), calls=%async_computation.4 | async-start | bytes 3211264 | tf_op jit(solution)/shard_map/all_to_all | solution.py:170
  226.4 85.8 %copy-start.76 = (f32[16]{0:T(128)}, f32[16]{0:T(128)S(1)}, u32[]{:S(2)}) copy-start(f32[16]{0:T(128)S(1)} %get-tuple-element.793) | copy-start | bytes 196
  229.9 34.8 %copy-start.2 = (f32[16,3,12544]{2,0,1:T(8,128)S(1)}, f32[16,3,12544]{2,0,1:T(8,128)}, u32[]{:S(2)}) copy-start(f32[16,3,12544]{2,0,1:T(8,128)} %get-tuple-element.509) | copy-start | bytes 7225348
  260.3 41.6 %all-to-all-start.3 = ((f32[4,8,12544]{2,1,0:T(8,128)}), f32[4,8,12544]{2,1,0:T(8,128)}, u32[]{:S(2)}, u32[]{:S(2)}) async-start(f32[4,8,12544]{2,1,0:T(8,128)} %fusion.177), calls=%async_computation.3 | async-start | bytes 3211264 | tf_op jit(solution)/shard_map/all_to_all | solution.py:169
  267.1 34.8 %copy-start.56 = (f32[8,12544]{1,0:T(8,128)S(1)}, f32[8,12544]{1,0:T(8,128)}, u32[]{:S(2)}) copy-start(f32[8,12544]{1,0:T(8,128)} %fusion.249) | copy-start | bytes 1204228
  307.0 40.8 %all-to-all-start.7 = ((f32[4,8,12544]{2,1,0:T(8,128)}), f32[4,8,12544]{2,1,0:T(8,128)S(1)}, u32[]{:S(2)}, u32[]{:S(2)}) async-start(f32[4,8,12544]{2,1,0:T(8,128)} %bitcast.1784), calls=%async_computation.7 | async-start | bytes 3211264 | tf_op jit(solution)/shard_map/all_to_all | solution.py:141
  357.2 20.8 %copy-start.10 = (f32[16,3,12544]{2,0,1:T(8,128)}, f32[16,3,12544]{2,0,1:T(8,128)S(1)}, u32[]{:S(2)}) copy-start(f32[16,3,12544]{2,0,1:T(8,128)S(1)} %get-tuple-element.485) | copy-start | bytes 7225348
  433.6 16.4 %copy-start.53 = (bf16[16,1,12544]{2,0,1:T(8,128)(2,1)S(1)}, bf16[16,1,12544]{2,0,1:T(8,128)(2,1)}, u32[]{:S(2)}) copy-start(bf16[16,1,12544]{2,0,1:T(8,128)(2,1)} %copy-done.51) | copy-start | bytes 1204228
  442.0 13.3 %all-to-all-start.10 = ((f32[4,8,8]{1,2,0:T(8,128)}), f32[4,8,8]{1,2,0:T(8,128)S(1)}, u32[]{:S(2)}, u32[]{:S(2)}) async-start(f32[4,8,8]{1,2,0:T(8,128)} %copy.1203), calls=%async_computation.10 | async-start | bytes 32768 | tf_op jit(solution)/shard_map/all_to_all | solution.py:171
  449.9 14.3 %copy-start.111 = (f32[7]{0:T(128)S(1)}, f32[7]{0:T(128)}, u32[]{:S(2)}) copy-start(f32[7]{0:T(128)} %constant.89.clone) | copy-start | bytes 88
  452.7 33.5 %copy-start.5 = (f32[16,3,12544]{2,0,1:T(8,128)S(1)}, f32[16,3,12544]{2,0,1:T(8,128)}, u32[]{:S(2)}) copy-start(f32[16,3,12544]{2,0,1:T(8,128)} %get-tuple-element.876) | copy-start | bytes 7225348
  466.2 10.6 %all-to-all-start.11 = ((f32[4,8,7]{2,1,0:T(8,128)}), f32[4,8,7]{2,1,0:T(8,128)S(1)}, u32[]{:S(2)}, u32[]{:S(2)}) async-start(f32[4,8,7]{2,1,0:T(8,128)} %bitcast.322), calls=%async_computation.11 | async-start | bytes 32768 | tf_op jit(solution)/shard_map/all_to_all | solution.py:148
  476.8 41.0 %all-to-all-start.9 = ((f32[4,8,12544]{2,1,0:T(8,128)}), f32[4,8,12544]{2,1,0:T(8,128)}, u32[]{:S(2)}, u32[]{:S(2)}) async-start(f32[4,8,12544]{2,1,0:T(8,128)} %fusion.125), calls=%async_computation.9 | async-start | bytes 3211264 | tf_op jit(solution)/shard_map/all_to_all | solution.py:170
  484.9 148.2 %copy-start.66 = (f32[16]{0:T(128)}, f32[16]{0:T(128)S(1)}, u32[]{:S(2)}) copy-start(f32[16]{0:T(128)S(1)} %get-tuple-element.770) | copy-start | bytes 196
  485.5 147.6 %copy-start.68 = (f32[16]{0:T(128)}, f32[16]{0:T(128)S(1)}, u32[]{:S(2)}) copy-start(f32[16]{0:T(128)S(1)} %get-tuple-element.771) | copy-start | bytes 196
  485.5 147.6 %copy-start.70 = (f32[16]{0:T(128)}, f32[16]{0:T(128)S(1)}, u32[]{:S(2)}) copy-start(f32[16]{0:T(128)S(1)} %get-tuple-element.773) | copy-start | bytes 196
  486.0 147.1 %copy-start.72 = (f32[16]{0:T(128)}, f32[16]{0:T(128)S(1)}, u32[]{:S(2)}) copy-start(f32[16]{0:T(128)S(1)} %get-tuple-element.774) | copy-start | bytes 196
  486.0 147.1 %copy-start.74 = (f32[16]{0:T(128)}, f32[16]{0:T(128)S(1)}, u32[]{:S(2)}) copy-start(f32[16]{0:T(128)S(1)} %get-tuple-element.776) | copy-start | bytes 196
  488.0 34.2 %copy-start.3 = (f32[16,3,12544]{2,0,1:T(8,128)S(1)}, f32[16,3,12544]{2,0,1:T(8,128)}, u32[]{:S(2)}) copy-start(f32[16,3,12544]{2,0,1:T(8,128)} %get-tuple-element.509) | copy-start | bytes 7225348
  517.8 41.6 %all-to-all-start.8 = ((f32[4,8,12544]{2,1,0:T(8,128)}), f32[4,8,12544]{2,1,0:T(8,128)}, u32[]{:S(2)}, u32[]{:S(2)}) async-start(f32[4,8,12544]{2,1,0:T(8,128)} %fusion.158), calls=%async_computation.8 | async-start | bytes 3211264 | tf_op jit(solution)/shard_map/all_to_all | solution.py:169
  524.6 34.7 %copy-start.55 = (f32[8,12544]{1,0:T(8,128)S(1)}, f32[8,12544]{1,0:T(8,128)}, u32[]{:S(2)}) copy-start(f32[8,12544]{1,0:T(8,128)} %fusion.226) | copy-start | bytes 1204228
  564.5 40.8 %all-to-all-start.12 = ((f32[4,8,12544]{2,1,0:T(8,128)}), f32[4,8,12544]{2,1,0:T(8,128)S(1)}, u32[]{:S(2)}, u32[]{:S(2)}) async-start(f32[4,8,12544]{2,1,0:T(8,128)} %bitcast.1785), calls=%async_computation.12 | async-start | bytes 3211264 | tf_op jit(solution)/shard_map/all_to_all | solution.py:141
  614.4 18.7 %copy-start.6 = (f32[16,3,12544]{2,0,1:T(8,128)}, f32[16,3,12544]{2,0,1:T(8,128)S(1)}, u32[]{:S(2)}) copy-start(f32[16,3,12544]{2,0,1:T(8,128)S(1)} %get-tuple-element.467) | copy-start | bytes 7225348
  664.3 33.2 %copy-start.54 = (bf16[16,1,12544]{2,0,1:T(8,128)(2,1)S(1)}, bf16[16,1,12544]{2,0,1:T(8,128)(2,1)}, u32[]{:S(2)}) copy-start(bf16[16,1,12544]{2,0,1:T(8,128)(2,1)} %copy-done.51) | copy-start | bytes 1204228
  694.2 8.8 %all-to-all-start.15 = ((f32[4,8,8]{1,2,0:T(8,128)}), f32[4,8,8]{1,2,0:T(8,128)S(1)}, u32[]{:S(2)}, u32[]{:S(2)}) async-start(f32[4,8,8]{1,2,0:T(8,128)} %copy.1233), calls=%async_computation.15 | async-start | bytes 32768 | tf_op jit(solution)/shard_map/all_to_all | solution.py:171
  703.1 40.5 %all-to-all-start.14 = ((f32[4,8,12544]{2,1,0:T(8,128)}), f32[4,8,12544]{2,1,0:T(8,128)}, u32[]{:S(2)}, u32[]{:S(2)}) async-start(f32[4,8,12544]{2,1,0:T(8,128)} %fusion.128), calls=%async_computation.14 | async-start | bytes 3211264 | tf_op jit(solution)/shard_map/all_to_all | solution.py:170
  715.2 32.7 %copy-start.124 = (f32[16]{0:T(128)S(1)}, f32[16]{0:T(128)}, u32[]{:S(2)}) copy-start(f32[16]{0:T(128)} %get-tuple-element.337) | copy-start | bytes 196
  715.2 32.7 %copy-start.125 = (f32[16]{0:T(128)S(1)}, f32[16]{0:T(128)}, u32[]{:S(2)}) copy-start(f32[16]{0:T(128)} %get-tuple-element.338) | copy-start | bytes 196
  715.2 32.7 %copy-start.140 = (f32[16]{0:T(128)S(1)}, f32[16]{0:T(128)}, u32[]{:S(2)}) copy-start(f32[16]{0:T(128)} %get-tuple-element.405) | copy-start | bytes 196
  715.2 32.7 %copy-start.141 = (f32[16]{0:T(128)S(1)}, f32[16]{0:T(128)}, u32[]{:S(2)}) copy-start(f32[16]{0:T(128)} %get-tuple-element.406) | copy-start | bytes 196
  715.2 32.7 %copy-start.142 = (f32[16]{0:T(128)S(1)}, f32[16]{0:T(128)}, u32[]{:S(2)}) copy-start(f32[16]{0:T(128)} %get-tuple-element.408) | copy-start | bytes 196
  715.2 32.7 %copy-start.143 = (f32[16]{0:T(128)S(1)}, f32[16]{0:T(128)}, u32[]{:S(2)}) copy-start(f32[16]{0:T(128)} %get-tuple-element.418) | copy-start | bytes 196
  715.3 32.7 %copy-start.144 = (f32[16]{0:T(128)S(1)}, f32[16]{0:T(128)}, u32[]{:S(2)}) copy-start(f32[16]{0:T(128)} %get-tuple-element.420) | copy-start | bytes 196
  715.3 32.7 %copy-start.145 = (f32[16]{0:T(128)S(1)}, f32[16]{0:T(128)}, u32[]{:S(2)}) copy-start(f32[16]{0:T(128)} %get-tuple-element.425) | copy-start | bytes 196
  715.3 32.7 %copy-start.146 = (f32[16]{0:T(128)S(1)}, f32[16]{0:T(128)}, u32[]{:S(2)}) copy-start(f32[16]{0:T(128)} %get-tuple-element.426) | copy-start | bytes 196
  715.3 32.7 %copy-start.225 = (f32[16]{0:T(128)S(1)}, f32[16]{0:T(128)}, u32[]{:S(2)}) copy-start(f32[16]{0:T(128)} %get-tuple-element.431) | copy-start | bytes 196
  715.3 32.7 %copy-start.226 = (f32[16]{0:T(128)S(1)}, f32[16]{0:T(128)}, u32[]{:S(2)}) copy-start(f32[16]{0:T(128)} %get-tuple-element.432) | copy-start | bytes 196
  715.3 32.8 %copy-start.118 = (f32[16]{0:T(128)S(1)}, f32[16]{0:T(128)}, u32[]{:S(2)}) copy-start(f32[16]{0:T(128)} %get-tuple-element.300) | copy-start | bytes 196
  715.3 32.8 %copy-start.119 = (f32[16]{0:T(128)S(1)}, f32[16]{0:T(128)}, u32[]{:S(2)}) copy-start(f32[16]{0:T(128)} %get-tuple-element.302) | copy-start | bytes 196
  715.3 32.8 %copy-start.120 = (f32[16]{0:T(128)S(1)}, f32[16]{0:T(128)}, u32[]{:S(2)}) copy-start(f32[16]{0:T(128)} %get-tuple-element.303) | copy-start | bytes 196
  715.3 32.8 %copy-start.121 = (f32[16]{0:T(128)S(1)}, f32[16]{0:T(128)}, u32[]{:S(2)}) copy-start(f32[16]{0:T(128)} %get-tuple-element.305) | copy-start | bytes 196
  715.3 32.8 %copy-start.122 = (f32[16]{0:T(128)S(1)}, f32[16]{0:T(128)}, u32[]{:S(2)}) copy-start(f32[16]{0:T(128)} %get-tuple-element.306) | copy-start | bytes 196
  715.4 32.8 %copy-start.123 = (f32[16]{0:T(128)S(1)}, f32[16]{0:T(128)}, u32[]{:S(2)}) copy-start(f32[16]{0:T(128)} %get-tuple-element.308) | copy-start | bytes 196
  715.4 32.8 %copy-start.223 = (f32[16]{0:T(128)S(1)}, f32[16]{0:T(128)}, u32[]{:S(2)}) copy-start(f32[16]{0:T(128)} %get-tuple-element.246) | copy-start | bytes 196
  715.4 32.8 %copy-start.224 = (f32[16]{0:T(128)S(1)}, f32[16]{0:T(128)}, u32[]{:S(2)}) copy-start(f32[16]{0:T(128)} %get-tuple-element.247) | copy-start | bytes 196
  715.4 32.8 %copy-start.244 = (f32[16]{0:T(128)S(1)}, f32[16]{0:T(128)}, u32[]{:S(2)}) copy-start(f32[16]{0:T(128)} %get-tuple-element.463) | copy-start | bytes 196
  715.4 35.1 %copy-start.252 = (f32[8]{0:T(128)S(1)}, f32[8]{0:T(128)}, u32[]{:S(2)}) copy-start(f32[8]{0:T(128)} %convolution_bitcast_fusion.3) | copy-start | bytes 100
  715.4 41.7 %copy-start.112 = (f32[7]{0:T(128)S(1)}, f32[7]{0:T(128)}, u32[]{:S(2)}) copy-start(f32[7]{0:T(128)} %constant.89.clone) | copy-start | bytes 88
  715.4 41.7 %copy-start.115 = (f32[16]{0:T(128)S(1)}, f32[16]{0:T(128)}, u32[]{:S(2)}) copy-start(f32[16]{0:T(128)} %copy-done.113) | copy-start | bytes 196
  715.4 42.4 %copy-start.109 = (f32[7]{0:T(128)S(1)}, f32[7]{0:T(128)}, u32[]{:S(2)}) copy-start(f32[7]{0:T(128)} %constant.88.clone) | copy-start | bytes 88
  743.5 41.6 %all-to-all-start.13 = ((f32[4,8,12544]{2,1,0:T(8,128)}), f32[4,8,12544]{2,1,0:T(8,128)}, u32[]{:S(2)}, u32[]{:S(2)}) async-start(f32[4,8,12544]{2,1,0:T(8,128)} %fusion.139), calls=%async_computation.13 | async-start | bytes 3211264 | tf_op jit(solution)/shard_map/all_to_all | solution.py:169
  (205 other events, 735.2 us)
where the time goes:
time: 797 us; the launch traced here: 788 us
  waiting for transfers between devices  289 us (36%)
  matrix products  253 us (32%)
  other arithmetic  107 us (13%)
  starting transfers between devices  68.4 us (9%)
  local copies, waits for them, and re-layouts  49 us (6%)
  blocking collectives  18.3 us (2%)
    dot_general x12, matrix products, outer_sum(): jnp.einsum('jp,kp->jk', left, right, precision=lax.Precision.HIGHEST, pre...  202 us
    all_to_all x3, waiting for transfers between devices, per_device(): lax.all_to_all(log_depth[pick].reshape(blocks, slots, pix_dev), 'img', sp...  94.9 us
    all_to_all x3, waiting for transfers between devices, per_device(): lax.all_to_all(back_z, 'img', split_axis=0, concat_axis=0, tiled=True)  89.9 us
    all_to_all x3, waiting for transfers between devices, per_device(): lax.all_to_all(back_curv, 'img', split_axis=0, concat_axis=0, tiled=True)  88.3 us
    dot_general x31, matrix products, matmul(): jnp.dot(left, right, precision=lax.Precision.HIGHEST, preferred_element_t...  50.4 us
    add x12, other arithmetic, apply_matrix(): mat[row, 0] * vec[0] + mat[row, 1] * vec[1] + mat[row, 2] * vec[2]  24.8 us
    psum x3, blocking collectives, per_device(): lax.psum((grad_i, weight_i, grad_p, weight_p), 'pair')  18.3 us
  transfers between devices with their start and end apart: 16, of which 13 were waited for; matrix products, arithmetic and copies ran while one was open for 12% of the time, Pallas kernels for 0%

commit v1 on v0

v1 whole, which is shorter than its diff:
```python
import functools

import jax
import jax.numpy as jnp
from jax import lax
from jax.experimental import pallas as pl
from jax.experimental.pallas import tpu as pltpu
from jax.sharding import PartitionSpec as P

SIDE = 224
STEPS = 3
LANES = 128
CHUNK = 16
MESH = pl.DeviceIdType.MESH
ROWS = 40
SYM = ((0, 0), (0, 1), (0, 2), (1, 1), (1, 2), (2, 2))


def rot_rows(w):
    norm = w[0] * w[0] + w[1] * w[1] + w[2] * w[2]
    k = 2.0 / (1.0 + norm)
    cross = [[None, -w[2], w[1]], [w[2], None, -w[0]], [-w[1], w[0], None]]
    out = []
    for i in range(3):
        line = []
        for j in range(3):
            if i == j:
                line.append(1.0 + k * (w[i] * w[i] - norm))
            else:
                line.append(k * (cross[i][j] + w[i] * w[j]))
        out.append(line)
    return out


def rot_grad_rows(w, g):
    norm = w[0] * w[0] + w[1] * w[1] + w[2] * w[2]
    k = 2.0 / (1.0 + norm)
    trace = g[0][0] + g[1][1] + g[2][2]
    skew = [g[2][1] - g[1][2], g[0][2] - g[2][0], g[1][0] - g[0][1]]
    lin = [sum(g[i][j] * w[j] for j in range(3)) for i in range(3)]
    both = [lin[i] + sum(g[j][i] * w[j] for j in range(3)) for i in range(3)]
    value = sum(w[i] * (skew[i] + lin[i]) for i in range(3)) - norm * trace
    return [
        k * (skew[i] + both[i] - 2.0 * w[i] * trace) - k * k * w[i] * value for i in range(3)
    ]


def coef_rows(st):
    factor = jnp.exp(st[0])
    re = rot_rows(st[1:4])
    rg = rot_rows(st[8:11])
    gap = [st[4 + i] - st[11 + i] for i in range(3)]
    rows = []
    for j in range(3):
        for k in range(3):
            rows.append(factor * sum(rg[i][j] * re[i][k] for i in range(3)))
    for j in range(3):
        rows.append(sum(rg[i][j] * gap[i] for i in range(3)))
    rows.append(jnp.exp(-st[7]))
    zero = jnp.zeros_like(rows[0])
    return rows + [zero] * 3


def update_rows(st, mom, same, swap):
    factor = jnp.exp(st[0])
    u, w = st[1:4], st[8:11]
    re, rg = rot_rows(u), rot_rows(w)
    gap = [st[11 + i] - st[4 + i] for i in range(3)]
    d1 = mom[0:3]
    tx = [mom[3 + 3 * j : 6 + 3 * j] for j in range(3)]
    s0 = mom[16]
    s1 = mom[17:20]
    s2, dd = {}, {}
    for n, (i, j) in enumerate(SYM):
        s2[i, j] = s2[j, i] = mom[20 + n]
        dd[i, j] = dd[j, i] = mom[32 + n]
    sre = [[factor * re[i][j] for j in range(3)] for i in range(3)]

    def dot(left, right):
        return left[0] * right[0] + left[1] * right[1] + left[2] * right[2]

    shift = [2.0 * (dot(rg[i], d1) + gap[i] * s0 - dot(sre[i], s1)) for i in range(3)]
    mx = [
        [
            2.0
            * (
                dot(rg[i], [tx[j][k] for j in range(3)])
                + gap[i] * s1[k]
                - dot(sre[i], [s2[j, k] for j in range(3)])
            )
            for k in range(3)
        ]
        for i in range(3)
    ]
    mc = [
        [
            2.0
            * (
                dot(rg[i], [dd[j, k] for j in range(3)])
                + gap[i] * d1[k]
                - dot(sre[i], tx[k])
            )
            for k in range(3)
        ]
        for i in range(3)
    ]
    d_scale = -sum(mx[i][k] * sre[i][k] for i in range(3) for k in range(3))
    d_spin = rot_grad_rows(u, [[-factor * mx[i][k] for k in range(3)] for i in range(3)])
    d_turn = rot_grad_rows(w, mc)
    d_focal = -sum(rg[i][j] * mc[i][j] for i in range(3) for j in range(2))
    grads_p = jnp.concatenate([d_scale] + d_spin + [-x for x in shift] + [s0], 0)
    grads_i = jnp.concatenate([d_focal] + d_turn + shift + [s0], 0)
    grads_p = grads_p + swap(grads_p)
    grads_i = jnp.dot(
        grads_i,
        same,
        precision=lax.Precision.HIGHEST,
        preferred_element_type=jnp.float32,
    )
    rate_p = (0.05, 0.02, 0.02, 0.02, 0.3, 0.3, 0.3)
    rate_i = (0.1, 0.02, 0.02, 0.02, 0.3, 0.3, 0.3)
    down_p = 1.0 / (grads_p[7:8] + 1.0)
    down_i = 1.0 / (grads_i[7:8] + 1.0)
    new = [st[i] - rate_p[i] * grads_p[i : i + 1] * down_p for i in range(7)]
    new += [st[7 + i] - rate_i[i] * grads_i[i : i + 1] * down_i for i in range(7)]
    return new


def step_kernel(first, meta, rep, coef, own, far, z_ref, a_ref, b_ref, *rest):
    if first:
        z_out, mom_out, dc, total, weights = rest
    else:
        before, z_out, mom_out, dc, total, weights = rest
    images, rows, _ = z_ref.shape
    views = coef.shape[1]
    own_count, far_count = own.shape[0], meta.shape[1] - own.shape[0]
    lane = lax.broadcasted_iota(jnp.int32, (1, views), 1)
    cuts = [pl.ds(c * CHUNK, CHUNK) for c in range(rows // CHUNK)]

    mom_out[...] = jnp.zeros_like(mom_out)
    if not first:
        mom_out[16:32, :] = before[16:32, :]

    def half(x):
        return x[0:8] + x[8:16]

    def put(row, sums, column):
        lines = [jnp.sum(x, 0, keepdims=True) for x in sums]
        count = -(-len(lines) // 8) * 8
        lines += [jnp.zeros_like(lines[0])] * (count - len(lines))
        value = jnp.sum(jnp.concatenate(lines, 0), 1, keepdims=True)
        mom_out[row : row + count, :] += jnp.where(lane == column, value, 0.0)

    def prepare(g, _):
        inv = coef[12, rep[g]]
        for cut in cuts:
            d = jnp.exp(z_ref[g, cut, :])
            near = d * inv
            dc[g, 0, cut, :] = near * a_ref[cut, :]
            dc[g, 1, cut, :] = near * b_ref[cut, :]
            dc[g, 2, cut, :] = d
            total[g, cut, :] = jnp.zeros((CHUNK, LANES), jnp.float32)
            weights[g, cut, :] = jnp.zeros((CHUNK, LANES), jnp.float32)
        return 0

    lax.fori_loop(0, images, prepare, 0)

    def view(data, slot, g, column):
        q = [[coef[3 * j + k, column] for k in range(3)] for j in range(3)]
        p = [coef[9 + j, column] for j in range(3)]
        sums = None
        consts = None
        for cut in cuts:
            x = [data[slot, k, cut, :].astype(jnp.float32) for k in range(3)]
            w = data[slot, 3, cut, :].astype(jnp.float32)
            y = [dc[g, j, cut, :] * w for j in range(3)]
            t = [[y[j] * x[k] for k in range(3)] for j in range(3)]
            pull = p[0] * y[0] + p[1] * y[1] + p[2] * y[2]
            for j in range(3):
                for k in range(3):
                    pull = pull + q[j][k] * t[j][k]
            total[g, cut, :] += pull
            weights[g, cut, :] += w
            new = [half(v) for v in y] + [half(t[j][k]) for j in range(3) for k in range(3)]
            sums = new if sums is None else [s + v for s, v in zip(sums, new)]
            if first:
                wx = [w * x[k] for k in range(3)]
                new = [half(w)] + [half(v) for v in wx]
                new += [half(wx[i] * x[j]) for i, j in SYM]
                consts = new if consts is None else [s + v for s, v in zip(consts, new)]
        put(0, sums, column)
        if first:
            put(16, consts, column)

    def own_view(i, _):
        view(own, meta[1, i], meta[2, i], meta[3, i])
        return 0

    lax.fori_loop(0, own_count, own_view, 0)

    def far_view(i, _):
        at = own_count + i

        @pl.when(meta[0, at] > 0)
        def _():
            view(far, meta[1, at], meta[2, at], meta[3, at])

        return 0

    lax.fori_loop(0, far_count, far_view, 0)

    def finish(g, _):
        sums = None
        for cut in cuts:
            c = [dc[g, j, cut, :] for j in range(3)]
            w = weights[g, cut, :]
            wc = [w * c[j] for j in range(3)]
            twice = 2.0 * (wc[0] * c[0] + wc[1] * c[1] + wc[2] * c[2])
            z_out[g, cut, :] = z_ref[g, cut, :] - (twice - 2.0 * total[g, cut, :]) / (twice + 1.0)
            new = [half(wc[i] * c[j]) for i, j in SYM]
            sums = new if sums is None else [s + v for s, v in zip(sums, new)]
        put(32, sums, rep[g])
        return 0

    lax.fori_loop(0, images, finish, 0)


def run_step(first, meta, rep, coef, own, far, z, a, b, before):
    images, rows, _ = z.shape
    views = coef.shape[1]
    smem = pl.BlockSpec(memory_space=pltpu.SMEM)
    vmem = pl.BlockSpec(memory_space=pltpu.VMEM)
    args = [meta, rep, coef, own, far, z, a, b] + ([] if first else [before])
    return pl.pallas_call(
        functools.partial(step_kernel, first),
        out_shape=(
            jax.ShapeDtypeStruct(z.shape, jnp.float32),
            jax.ShapeDtypeStruct((ROWS, views), jnp.float32),
        ),
        in_specs=[smem] * 3 + [vmem] * (len(args) - 3),
        out_specs=(vmem, vmem),
        scratch_shapes=[
            pltpu.VMEM((images, 3, rows, LANES), jnp.float32),
            pltpu.VMEM((images, rows, LANES), jnp.float32),
            pltpu.VMEM((images, rows, LANES), jnp.float32),
        ],
        compiler_params=pltpu.CompilerParams(vmem_limit_bytes=32 * 1024 * 1024),
    )(*args)


def share_kernel(
    n_pair, n_img, mom, state, same, state_out, coef_out, buf1, buf2, s1, r1, s2, r2
):
    views = mom.shape[1]
    stages = (("pair", n_pair, buf1, s1, r1), ("img", n_img, buf2, s2, r2))
    barrier = pltpu.get_barrier_semaphore()
    for axis, size, _, _, _ in stages:
        me = lax.axis_index(axis)
        for k in range(1, size):
            peer = lax.rem(me + k, size)
            pl.semaphore_signal(barrier, inc=1, device_id={axis: peer}, device_id_type=MESH)
    pl.semaphore_wait(barrier, n_pair + n_img - 2)

    value = mom[...]
    for axis, size, buf, send, recv in stages:
        me = lax.axis_index(axis)
        buf[me] = value
        copies = []
        for k in range(1, size):
            peer = lax.rem(me + k, size)
            copy = pltpu.make_async_remote_copy(
                src_ref=buf.at[me],
                dst_ref=buf.at[me],
                send_sem=send.at[k],
                recv_sem=recv.at[me],
                device_id={axis: peer},
                device_id_type=MESH,
            )
            copy.start()
            copies.append(copy)
        for k in range(1, size):
            peer = lax.rem(me + k, size)
            pltpu.make_async_remote_copy(
                src_ref=buf.at[peer],
                dst_ref=buf.at[peer],
                send_sem=send.at[k],
                recv_sem=recv.at[peer],
                device_id={axis: peer},
                device_id_type=MESH,
            ).wait_recv()
        value = buf[0]
        for k in range(1, size):
            value = value + buf[k]
        for copy in copies:
            copy.wait_send()

    moments = [value[i : i + 1] for i in range(ROWS)]
    st = [state[i : i + 1, :] for i in range(14)]
    new = update_rows(st, moments, same[...], lambda x: pltpu.roll(x, views // 2, axis=1))
    zero = jnp.zeros_like(new[0])
    state_out[...] = jnp.concatenate(new + [zero] * 2, 0)
    coef_out[...] = jnp.concatenate(coef_rows(new), 0)


def run_share(n_pair, n_img, mom, state, same):
    views = mom.shape[1]
    vmem = pl.BlockSpec(memory_space=pltpu.VMEM)
    return pl.pallas_call(
        functools.partial(share_kernel, n_pair, n_img),
        out_shape=(
            jax.ShapeDtypeStruct((16, views), jnp.float32),
            jax.ShapeDtypeStruct((16, views), jnp.float32),
        ),
        in_specs=[vmem] * 3,
        out_specs=(vmem, vmem),
        scratch_shapes=[
            pltpu.VMEM((n_pair, ROWS, views), jnp.float32),
            pltpu.VMEM((n_img, ROWS, views), jnp.float32),
            pltpu.SemaphoreType.DMA((n_pair,)),
            pltpu.SemaphoreType.DMA((n_pair,)),
            pltpu.SemaphoreType.DMA((n_img,)),
            pltpu.SemaphoreType.DMA((n_img,)),
        ],
        compiler_params=pltpu.CompilerParams(collective_id=0, has_side_effects=True),
    )(mom, state, same)


def per_device(pair_images, pointmaps, confidence, log_depth, image_params, pair_params):
    pair_dev = pair_images.shape[0]
    img_dev, pix_dev = log_depth.shape
    blocks = lax.axis_size("img")
    n_pair = lax.axis_size("pair")
    slots = max(2, 2 * pair_dev // blocks)
    here = lax.axis_index("img")
    rows = -(-pix_dev // (LANES * CHUNK)) * CHUNK
    pad = rows * LANES - pix_dev

    pixel = lax.axis_index("pair") * pix_dev + jnp.arange(rows * LANES)
    coord_a = ((pixel % SIDE).astype(jnp.float32) - (SIDE - 1) / 2.0) / SIDE
    coord_b = ((pixel // SIDE).astype(jnp.float32) - (SIDE - 1) / 2.0) / SIDE
    coord_a = coord_a.reshape(rows, LANES)
    coord_b = coord_b.reshape(rows, LANES)

    target = pair_images[:, 1] // img_dev
    hits = (target[:, None] == jnp.arange(blocks)[None, :]).astype(jnp.int32)
    rank = jnp.sum(jnp.cumsum(hits, 0) * hits, 1) - 1
    place = target * slots + rank
    source = jnp.sum(
        (place[None, :] == jnp.arange(blocks * slots)[:, None]) * jnp.arange(pair_dev)[None, :], 1
    )

    packed = jnp.concatenate([pointmaps, confidence[:, :, None, :]], 2)
    packed = jnp.pad(packed, ((0, 0), (0, 0), (0, 0), (0, pad)))
    packed = packed.reshape(pair_dev, 2, 4, rows, LANES)
    own = packed[:, 0]
    send = packed[:, 1][source].reshape(blocks, slots, 4, rows, LANES)
    far = lax.all_to_all(send, "img", split_axis=0, concat_axis=0, tiled=True)
    far = far.reshape(blocks * slots, 4, rows, LANES)

    small = jnp.concatenate(
        [
            pair_images.astype(jnp.float32).reshape(-1),
            pair_params.reshape(-1),
            image_params.reshape(-1),
        ]
    )
    small = lax.all_gather(small, "img")
    cut1, cut2 = 2 * pair_dev, 9 * pair_dev
    all_ids = small[:, :cut1].astype(jnp.int32).reshape(blocks * pair_dev, 2)
    all_pairs = small[:, cut1:cut2].reshape(blocks * pair_dev, 7)
    all_images = small[:, cut2:].reshape(blocks * img_dev, 7)
    image_of = all_ids.T.reshape(-1)
    views = image_of.shape[0]
    pairs = views // 2
    same = (image_of[:, None] == image_of[None, :]).astype(jnp.float32)
    hot = (image_of[None, :] == jnp.arange(blocks * img_dev)[:, None]).astype(jnp.float32)
    by_view = jnp.dot(
        all_images.T, hot, precision=lax.Precision.HIGHEST, preferred_element_type=jnp.float32
    )
    state = jnp.concatenate(
        [jnp.tile(all_pairs.T, (1, 2)), by_view, jnp.zeros((2, views), jnp.float32)], 0
    )
    coef = jnp.concatenate(coef_rows([state[i : i + 1] for i in range(14)]), 0)

    far_ids = all_ids[:, 1].reshape(blocks, pair_dev)
    mine = (far_ids // img_dev == here).astype(jnp.int32)
    far_slot = jnp.arange(blocks)[:, None] * slots + jnp.cumsum(mine, 1) - 1
    mine = mine.reshape(-1)
    meta = jnp.stack(
        [
            jnp.concatenate([jnp.ones((pair_dev,), jnp.int32), mine]),
            jnp.concatenate([jnp.arange(pair_dev), jnp.maximum(far_slot.reshape(-1), 0)]),
            jnp.concatenate([pair_images[:, 0] - here * img_dev, far_ids.reshape(-1) % img_dev]),
            jnp.concatenate([here * pair_dev + jnp.arange(pair_dev), pairs + jnp.arange(pairs)]),
        ]
    ).astype(jnp.int32)
    local = image_of[None, :] == here * img_dev + jnp.arange(img_dev)[:, None]
    rep = jnp.max(jnp.where(local, jnp.arange(views)[None, :], -1), 1)
    seen = rep >= 0
    rep = jnp.maximum(rep, 0).astype(jnp.int32)

    z = jnp.pad(log_depth, ((0, 0), (0, pad))).reshape(img_dev, rows, LANES)
    before = None
    for step in range(STEPS):
        z, mom = run_step(step == 0, meta, rep, coef, own, far, z, coord_a, coord_b, before)
        before = mom
        state, coef = run_share(n_pair, blocks, mom, state, same)

    new_depth = z.reshape(img_dev, rows * LANES)[:, :pix_dev]
    new_pairs = lax.dynamic_slice(state, (0, here * pair_dev), (7, pair_dev)).T
    new_images = jnp.where(seen[:, None], state[7:14][:, rep].T, image_params)
    return (new_depth, new_images, new_pairs)


def solution(mesh):
    in_specs = (
        P(("groups", "img"), None),
        P(("groups", "img"), None, None, "pair"),
        P(("groups", "img"), None, "pair"),
        P(("groups", "img"), "pair"),
        P(("groups", "img"), None),
        P(("groups", "img"), None),
    )
    out_specs = (
        P(("groups", "img"), "pair"),
        P(("groups", "img"), None),
        P(("groups", "img"), None),
    )
    return jax.shard_map(
        per_device, mesh=mesh, in_specs=in_specs, out_specs=out_specs, check_vma=False
    )
```

time: 797 us -> 196 us (0.25); the launches traced: 788 us -> 197 us
  waiting for transfers between devices: 289 us -> 11.9 us
  matrix products: 253 us -> 0.19 us
  other arithmetic: 107 us -> 14.5 us
  Pallas kernels: 0 us -> 70.5 us
  starting transfers between devices: 68.4 us -> 6.46 us
  blocking collectives: 18.3 us -> 63.5 us
  local copies, waits for them, and re-layouts: 49 us -> 28.8 us
    all_to_all x16 -> x1, waiting for transfers between devices: 289 us -> 11.9 us  [per_device(): far = lax.all_to_all(send, 'img', split_axis=0, concat_axis=0, tiled=True)]
    dot_general x43 -> x1, matrix products: 253 us -> 0.19 us  [per_device(): jnp.dot(all_images.T, hot, precision=lax.Precision.HIGHEST, preferred_ele...]
    pallas_call x0 -> x6, Pallas kernels: none -> 70.5 us  [the longest x3 42.2 us: run_share(): pl.pallas_call(functools.partial(share_kernel, n_pair, n_img), out_shape=...]
    unnamed x0 -> x1, blocking collectives: none -> 63.5 us
    all_to_all x16 -> x1, starting transfers between devices: 68.4 us -> 6.46 us  [per_device(): far = lax.all_to_all(send, 'img', split_axis=0, concat_axis=0, tiled=True)]
    reduce_sum x20 -> x1, other arithmetic: 38 us -> 0.09 us  [per_device(): jnp.sum((place[None, :] == jnp.arange(blocks * slots)[:, None]) * jnp.ara...]
    add x24 -> x5, other arithmetic: 27.2 us -> 0.05 us  [the longest x2 0.03 us: coef_rows(): rows.append(sum((rg[i][j] * gap[i] for i in range(3))))]
    psum x3 -> x0, blocking collectives: 18.3 us -> none  [per_device(): lax.psum((grad_i, weight_i, grad_p, weight_p), 'pair')]
  transfers between devices with their start and end apart: 16 -> 1, of which waited for: 13 -> 1; matrix products, arithmetic and copies ran while one was open for 12% -> 3% of each run, Pallas kernels for 0% -> 0%
where the time goes in v1:
time: 196 us; the launch traced here: 197 us
  Pallas kernels  70.5 us (36%)
  blocking collectives  63.5 us (32%)
  local copies, waits for them, and re-layouts  28.8 us (15%)
  other arithmetic  14.5 us (7%)
  waiting for transfers between devices  11.9 us (6%)
  starting transfers between devices  6.46 us (3%)
    unnamed x1, blocking collectives  63.5 us
    pallas_call x3, Pallas kernels, run_share(): pl.pallas_call(functools.partial(share_kernel, n_pair, n_img), out_shape=...  42.2 us
    pallas_call x3, Pallas kernels, run_step(): pl.pallas_call(functools.partial(step_kernel, first), out_shape=(jax.Shap...  28.4 us
    all_to_all x1, waiting for transfers between devices, per_device(): far = lax.all_to_all(send, 'img', split_axis=0, concat_axis=0, tiled=True)  11.9 us
    concatenate x1, other arithmetic, per_device(): packed = jnp.concatenate([pointmaps, confidence[:, :, None, :]], 2)  9.48 us
    reshape x1, local copies, waits for them, and re-layouts, per_device(): packed = packed.reshape(pair_dev, 2, 4, rows, LANES)  9.16 us
    all_to_all x1, starting transfers between devices, per_device(): far = lax.all_to_all(send, 'img', split_axis=0, concat_axis=0, tiled=True)  6.46 us
    unnamed x30, local copies, waits for them, and re-layouts  5.59 us
  transfers between devices with their start and end apart: 1, of which 1 were waited for; matrix products, arithmetic and copies ran while one was open for 3% of the time, Pallas kernels for 0%

profile of v1, /device:TPU:0, one launch (start us, length us, event | category | flops | bytes accessed | tf_op | source)
XLA Modules:
  0.0 197.4 jit_solution(5335084120563255488)
XLA Ops:
  0.6 0.8 fusion.24
  1.5 0.2 select_reduce_fusion.1
  1.7 0.7 add_add_fusion.1
  2.4 0.1 select_reduce_fusion
  2.5 9.5 %fusion.2 = bf16[16,2,4,14336]{3,1,2,0:T(2,128)(2,1)} fusion(bf16[16,2,1,12544]{3,1,2,0:T(2,128)(2,1)} %bitcast.62, bf16[16,2,3,12544]{3,1,2,0:T(2,128)(2,1)} %param.7), kind=kLoop, calls=%fused_computation.5 | loop fusion | flops 12845056 | bytes 6881280 | tf_op jit(solution)/shard_map/concatenate | solution.py:352
  12.0 9.2 %reshape.892 = bf16[16,2,4,112,128]{4,3,1,2,0:T(8,128)(2,1)} reshape(bf16[16,2,4,14336]{3,1,2,0:T(2,128)(2,1)} %fusion.2) | data formatting | bytes 7340032 | tf_op jit(solution)/shard_map/reshape | solution.py:354
  21.1 3.6 %slice_bitcast_fusion = (bf16[16,4,112,128]{3,2,1,0:T(8,128)(2,1)}, bf16[16,4,112,128]{3,2,1,0:T(8,128)(2,1)S(1)}) fusion(bf16[16,2,4,112,128]{4,3,1,2,0:T(8,128)(2,1)} %reshape.892), kind=kLoop, calls=%fused_computation.6 | loop fusion | bytes 7340032 | tf_op jit(solution)/shard_map/squeeze | solution.py:356
  24.8 4.3 %gather_fusion = bf16[32,4,112,128]{3,2,1,0:T(8,128)(2,1)} fusion(bf16[16,4,112,128]{3,2,1,0:T(8,128)(2,1)} %get-tuple-element.60, s32[1024]{0:T(1024)S(1)} %pad_clamp_fusion.1), kind=kCustom, calls=%fused_computation | custom fusion | bytes 7340160 | tf_op jit(solution)/shard_map/gather | solution.py:356
  29.2 6.5 %all-to-all-start = ((bf16[4,8,4,112,128]{4,3,2,1,0:T(8,128)(2,1)}), bf16[4,8,4,112,128]{4,3,2,1,0:T(8,128)(2,1)}, u32[]{:S(2)}, u32[]{:S(2)}) async-start(bf16[4,8,4,112,128]{4,3,2,1,0:T(8,128)(2,1)} %bitcast.58), calls=%async_computation | async-start | bytes 7340032 | tf_op jit(solution)/shard_map/all_to_all | solution.py:357
  35.6 0.1 copy.29
  35.7 0.1 reshape.857
  35.8 0.1 copy.30
  35.9 0.1 reshape.858
  36.0 0.1 reshape.859
  36.1 0.6 dynamic-slice
  37.3 0.2 maximum_dynamic-update-slice_fusion
  37.5 63.5 %all-reduce.3 = f32[800]{0:T(1024)S(1)} all-reduce(f32[800]{0:T(1024)S(1)} %maximum_dynamic-update-slice_fusion), channel_id=2, replica_groups=mesh['groups'=2,'img'=4,'pair'=4] {'img'}, use_global_device_ids=true, to_apply=%add.3 | all-reduce | flops 800 | bytes 6400
  101.0 0.1 reshape.885
  101.2 0.1 reshape.860
  101.4 0.1 eq.88
  101.4 0.1 reshape.862
  101.5 0.1 reshape.861
  101.7 0.3 slice_reduce_fusion
  102.0 0.1 tile.43
  102.1 0.1 tile.45
  102.2 0.1 tile.47
  102.3 0.1 exp.23
  102.4 0.1 tile.37
  102.5 0.1 tile.39
  102.6 0.1 tile.41
  102.6 0.2 slice_reduce_fusion.6
  102.8 0.1 reshape_squeeze.6
  102.9 0.2 reduce_window_sum.22
  103.2 0.1 max.13
  103.3 0.1 copy.44
  103.4 0.1 tile.49
  103.5 0.1 pad.14.clone
  103.6 0.2 fusion.15
  104.2 0.1 add_bitcast_fusion
  104.3 0.2 select_reduce_fusion.2
  104.5 0.1 fusion.5
  104.6 0.7 maximum_maximum_fusion.state
  105.3 0.7 compare_convert_fusion.same
  106.0 11.9 %all-to-all-done = bf16[4,8,4,112,128]{4,3,2,1,0:T(8,128)(2,1)} async-done(((bf16[4,8,4,112,128]{4,3,2,1,0:T(8,128)(2,1)}), bf16[4,8,4,112,128]{4,3,2,1,0:T(8,128)(2,1)}, u32[]{:S(2)}, u32[]{:S(2)}) %all-to-all-start) | async-done | bytes 3670048 | tf_op jit(solution)/shard_map/all_to_all | solution.py:357
  117.9 10.4 %shard_map.85 = (f32[8,112,128]{2,1,0:T(8,128)S(1)}, f32[40,128]{1,0:T(8,128)S(1)}) custom-call(s32[4,80]{1,0:T(4,128)S(1)} %pad_add_fusion.meta, s32[8]{0:T(128)S(1)} %broadcast_maximum_fusion.rep, f32[16,128]{1,0:T(8,128)S(1)} %concatenate.33.coef, bf16[16,4,112,128]{3,2,1,0:T(8,128)(2,1)S(1)} %get-tuple-element.61.own, ...), custom_call_target="tpu_custom_call" | custom-call | tf_op jit(solution)/shard_map/pallas_call | solution.py:234
  128.3 0.6 copy-done.2
  128.9 18.2 %shard_map.86 = (f32[16,128]{1,0:T(8,128)}, f32[16,128]{1,0:T(8,128)}) custom-call(f32[40,128]{1,0:T(8,128)} %copy-done.2, f32[16,128]{1,0:T(8,128)} %maximum_maximum_fusion.state, f32[128,128]{1,0:T(8,128)} %compare_convert_fusion.same), custom_call_target="tpu_custom_call" | custom-call | tf_op jit(solution)/shard_map/pallas_call | solution.py:308
  147.1 0.7 copy-done.3
  147.9 0.7 copy-done.6
  148.6 9.0 %shard_map.87 = (f32[8,112,128]{2,1,0:T(8,128)S(1)}, f32[40,128]{1,0:T(8,128)S(1)}) custom-call(s32[4,80]{1,0:T(4,128)S(1)} %pad_add_fusion.meta, s32[8]{0:T(128)S(1)} %broadcast_maximum_fusion.rep, f32[16,128]{1,0:T(8,128)S(1)} %copy-done.6, bf16[16,4,112,128]{3,2,1,0:T(8,128)(2,1)S(1)} %get-tuple-element.61.own, bf16[32,4,112,128]{3,2,1,0:T(8,128)(2,1)} %bitcast.17.far, ...), custom_call_target="tpu_custom_call" | custom-call | tf_op jit(solution)/shard_map/pallas_call | solution.py:234
  157.5 0.6 copy-done
  158.1 12.0 %shard_map.88 = (f32[16,128]{1,0:T(8,128)}, f32[16,128]{1,0:T(8,128)}) custom-call(f32[40,128]{1,0:T(8,128)} %copy-done, f32[16,128]{1,0:T(8,128)} %get-tuple-element.18.state, f32[128,128]{1,0:T(8,128)} %compare_convert_fusion.same), custom_call_target="tpu_custom_call" | custom-call | tf_op jit(solution)/shard_map/pallas_call | solution.py:308
  170.1 0.7 copy-done.1
  170.8 0.7 copy-done.5
  171.5 9.0 %shard_map.89 = (f32[8,112,128]{2,1,0:T(8,128)S(1)}, f32[40,128]{1,0:T(8,128)S(1)}) custom-call(s32[4,80]{1,0:T(4,128)S(1)} %pad_add_fusion.meta, s32[8]{0:T(128)S(1)} %broadcast_maximum_fusion.rep, f32[16,128]{1,0:T(8,128)S(1)} %copy-done.5, bf16[16,4,112,128]{3,2,1,0:T(8,128)(2,1)S(1)} %get-tuple-element.61.own, bf16[32,4,112,128]{3,2,1,0:T(8,128)(2,1)} %bitcast.17.far, ...), custom_call_target="tpu_custom_call" | custom-call | tf_op jit(solution)/shard_map/pallas_call | solution.py:234
  180.5 0.6 copy-done.4
  181.1 12.0 %shard_map.90 = (f32[16,128]{1,0:T(8,128)}, f32[16,128]{1,0:T(8,128)}) custom-call(f32[40,128]{1,0:T(8,128)} %copy-done.4, f32[16,128]{1,0:T(8,128)} %get-tuple-element.23.state, f32[128,128]{1,0:T(8,128)} %compare_convert_fusion.same), custom_call_target="tpu_custom_call" | custom-call | tf_op jit(solution)/shard_map/pallas_call | solution.py:308
  193.1 0.7 slice.127
  193.8 0.1 copy.35
  193.9 1.3 dynamic-slice_bitcast_fusion
  195.3 0.1 copy.43
  195.4 0.8 slice.145
  196.2 0.6 gather_fusion.1
  196.8 0.7 broadcast_select_fusion
  (60 shorter events, 1.0 us)
Async XLA Ops:
  29.1 6.5 %copy-start.10 = (s32[16,2]{0,1:T(2,128)S(1)}, s32[16,2]{0,1:T(2,128)}, u32[]{:S(2)}) copy-start(s32[16,2]{0,1:T(2,128)} %param.6) | copy-start | bytes 388
  29.1 6.7 %copy-start.9 = (f32[16,7]{0,1:T(8,128)S(1)}, f32[16,7]{0,1:T(8,128)}, u32[]{:S(2)}) copy-start(f32[16,7]{0,1:T(8,128)} %param.11) | copy-start | bytes 1348
  29.1 6.8 %copy-start.8 = (f32[8,7]{1,0:T(8,128)S(1)}, f32[8,7]{1,0:T(8,128)}, u32[]{:S(2)}) copy-start(f32[8,7]{1,0:T(8,128)} %param.10) | copy-start | bytes 676
  29.1 6.9 %copy-start.11 = (u32[32]{0:T(128)S(1)}, u32[32]{0:T(128)}, u32[]{:S(2)}) copy-start(u32[32]{0:T(128)} %constant.123) | copy-start | bytes 388
  29.1 74.2 %copy-start.7 = (f32[8,12544]{1,0:T(8,128)S(1)}, f32[8,12544]{1,0:T(8,128)}, u32[]{:S(2)}) copy-start(f32[8,12544]{1,0:T(8,128)} %param.9) | copy-start | bytes 1204228
  29.2 88.8 %all-to-all-start = ((bf16[4,8,4,112,128]{4,3,2,1,0:T(8,128)(2,1)}), bf16[4,8,4,112,128]{4,3,2,1,0:T(8,128)(2,1)}, u32[]{:S(2)}, u32[]{:S(2)}) async-start(bf16[4,8,4,112,128]{4,3,2,1,0:T(8,128)(2,1)} %bitcast.58), calls=%async_computation | async-start | bytes 7340032 | tf_op jit(solution)/shard_map/all_to_all | solution.py:357
  128.3 0.6 copy-start.2
  147.1 0.7 copy-start.3
  147.9 0.7 copy-start.6
  157.5 0.6 copy-start
  170.1 0.7 copy-start.1
  170.8 0.7 copy-start.5
  180.5 0.6 copy-start.4

commit v2 on v1

--- a/solution.py
+++ b/solution.py
@@ -135,14 +135,34 @@
     views = coef.shape[1]
     own_count, far_count = own.shape[0], meta.shape[1] - own.shape[0]
     lane = lax.broadcasted_iota(jnp.int32, (1, views), 1)
+    whole = rows // CHUNK * CHUNK
+    left = rows - whole
     cuts = [pl.ds(c * CHUNK, CHUNK) for c in range(rows // CHUNK)]
+    if left:
+        cuts.append(pl.ds(whole, left))
 
     mom_out[...] = jnp.zeros_like(mom_out)
     if not first:
         mom_out[16:32, :] = before[16:32, :]
 
     def half(x):
-        return x[0:8] + x[8:16]
+        if x.shape[0] == 16:
+            return x[0:8] + x[8:16]
+        if x.shape[0] > 8:
+            more = jnp.zeros((16 - x.shape[0], LANES), jnp.float32)
+            return x[0:8] + jnp.concatenate([x[8:], more], 0)
+        if x.shape[0] == 8:
+            return x
+        return jnp.concatenate([x, jnp.zeros((8 - x.shape[0], LANES), jnp.float32)], 0)
+
+    def fields(data, slot, cut):
+        if cut.size == CHUNK:
+            return [
+                data[slot, pl.ds(k * whole + cut.start, CHUNK), :].astype(jnp.float32)
+                for k in range(4)
+            ]
+        tail = data[slot, 4 * whole :, :].astype(jnp.float32)
+        return [tail[k * left : (k + 1) * left] for k in range(4)]
 
     def put(row, sums, column):
         lines = [jnp.sum(x, 0, keepdims=True) for x in sums]
@@ -159,8 +179,8 @@
             dc[g, 0, cut, :] = near * a_ref[cut, :]
             dc[g, 1, cut, :] = near * b_ref[cut, :]
             dc[g, 2, cut, :] = d
-            total[g, cut, :] = jnp.zeros((CHUNK, LANES), jnp.float32)
-            weights[g, cut, :] = jnp.zeros((CHUNK, LANES), jnp.float32)
+            total[g, cut, :] = jnp.zeros((cut.size, LANES), jnp.float32)
+            weights[g, cut, :] = jnp.zeros((cut.size, LANES), jnp.float32)
         return 0
 
     lax.fori_loop(0, images, prepare, 0)
@@ -171,8 +191,7 @@
         sums = None
         consts = None
         for cut in cuts:
-            x = [data[slot, k, cut, :].astype(jnp.float32) for k in range(3)]
-            w = data[slot, 3, cut, :].astype(jnp.float32)
+            *x, w = fields(data, slot, cut)
             y = [dc[g, j, cut, :] * w for j in range(3)]
             t = [[y[j] * x[k] for k in range(3)] for j in range(3)]
             pull = p[0] * y[0] + p[1] * y[1] + p[2] * y[2]
@@ -223,6 +242,63 @@
         return 0
 
     lax.fori_loop(0, images, finish, 0)
+
+
+def pack_kernel(place, maps, conf, own, send, wide):
+    pairs, parts, rows, _, _ = maps.shape
+    whole = rows // CHUNK * CHUNK
+    left = rows - whole
+
+    def pair(i, _):
+        tails = [[], []]
+        for k in range(parts + 1):
+            both = maps[i, k] if k < parts else conf[i]
+            wide[k, 0 : 2 * rows, :] = both.astype(jnp.float32).reshape(2 * rows, LANES)
+            for v in range(2):
+                body = wide[k, pl.ds(v, whole, stride=2), :].astype(jnp.bfloat16)
+                if v == 0:
+                    own[i, k * whole : (k + 1) * whole, :] = body
+                else:
+                    send[place[i], k * whole : (k + 1) * whole, :] = body
+                if left:
+                    tails[v].append(wide[k, pl.ds(2 * whole + v, left, stride=2), :])
+        if left:
+            start = (parts + 1) * whole
+            spare = tail_rows(rows) - (parts + 1) * left
+            for v in range(2):
+                lines = tails[v]
+                if spare:
+                    lines = lines + [jnp.zeros((spare, LANES), jnp.float32)]
+                tail = jnp.concatenate(lines, 0).astype(jnp.bfloat16)
+                if v == 0:
+                    own[i, start:, :] = tail
+                else:
+                    send[place[i], start:, :] = tail
+        return 0
+
+    lax.fori_loop(0, pairs, pair, 0)
+
+
+def tail_rows(rows):
+    return -(-4 * (rows % CHUNK) // CHUNK) * CHUNK
+
+
+def run_pack(place, slots, maps, conf):
+    pairs, parts, rows, _, _ = maps.shape
+    high = (parts + 1) * (rows // CHUNK * CHUNK) + tail_rows(rows)
+    smem = pl.BlockSpec(memory_space=pltpu.SMEM)
+    vmem = pl.BlockSpec(memory_space=pltpu.VMEM)
+    return pl.pallas_call(
+        pack_kernel,
+        out_shape=(
+            jax.ShapeDtypeStruct((pairs, high, LANES), jnp.bfloat16),
+            jax.ShapeDtypeStruct((slots, high, LANES), jnp.bfloat16),
+        ),
+        in_specs=[smem, vmem, vmem],
+        out_specs=(vmem, vmem),
+        scratch_shapes=[pltpu.VMEM((parts + 1, 2 * rows + 4, LANES), jnp.float32)],
+        compiler_params=pltpu.CompilerParams(vmem_limit_bytes=48 * 1024 * 1024),
+    )(place, maps, conf)
 
 
 def run_step(first, meta, rep, coef, own, far, z, a, b, before):
@@ -332,8 +408,7 @@
     n_pair = lax.axis_size("pair")
     slots = max(2, 2 * pair_dev // blocks)
     here = lax.axis_index("img")
-    rows = -(-pix_dev // (LANES * CHUNK)) * CHUNK
-    pad = rows * LANES - pix_dev
+    rows = pix_dev // LANES
 
     pixel = lax.axis_index("pair") * pix_dev + jnp.arange(rows * LANES)
     coord_a = ((pixel % SIDE).astype(jnp.float32) - (SIDE - 1) / 2.0) / SIDE
@@ -345,17 +420,13 @@
     hits = (target[:, None] == jnp.arange(blocks)[None, :]).astype(jnp.int32)
     rank = jnp.sum(jnp.cumsum(hits, 0) * hits, 1) - 1
     place = target * slots + rank
-    source = jnp.sum(
-        (place[None, :] == jnp.arange(blocks * slots)[:, None]) * jnp.arange(pair_dev)[None, :], 1
-    )
-
-    packed = jnp.concatenate([pointmaps, confidence[:, :, None, :]], 2)
-    packed = jnp.pad(packed, ((0, 0), (0, 0), (0, 0), (0, pad)))
-    packed = packed.reshape(pair_dev, 2, 4, rows, LANES)
-    own = packed[:, 0]
-    send = packed[:, 1][source].reshape(blocks, slots, 4, rows, LANES)
+    maps = pointmaps.reshape(pair_dev, 2, 3, rows, LANES).transpose(0, 2, 3, 1, 4)
+    conf = confidence.reshape(pair_dev, 2, rows, LANES).transpose(0, 2, 1, 3)
+    own, send = run_pack(place.astype(jnp.int32), blocks * slots, maps, conf)
+    high = own.shape[1]
+    send = send.reshape(blocks, slots, high, LANES)
     far = lax.all_to_all(send, "img", split_axis=0, concat_axis=0, tiled=True)
-    far = far.reshape(blocks * slots, 4, rows, LANES)
+    far = far.reshape(blocks * slots, high, LANES)
 
     small = jnp.concatenate(
         [
@@ -399,14 +470,14 @@
     seen = rep >= 0
     rep = jnp.maximum(rep, 0).astype(jnp.int32)
 
-    z = jnp.pad(log_depth, ((0, 0), (0, pad))).reshape(img_dev, rows, LANES)
+    z = log_depth.reshape(img_dev, rows, LANES)
     before = None
     for step in range(STEPS):
         z, mom = run_step(step == 0, meta, rep, coef, own, far, z, coord_a, coord_b, before)
         before = mom
         state, coef = run_share(n_pair, blocks, mom, state, same)
 
-    new_depth = z.reshape(img_dev, rows * LANES)[:, :pix_dev]
+    new_depth = z.reshape(img_dev, pix_dev)
     new_pairs = lax.dynamic_slice(state, (0, here * pair_dev), (7, pair_dev)).T
     new_images = jnp.where(seen[:, None], state[7:14][:, rep].T, image_params)
     return (new_depth, new_images, new_pairs)

time: 196 us -> 178 us (0.908); the launches traced: 197 us -> 176 us
  other arithmetic: 14.5 us -> 4.93 us
  blocking collectives: 63.5 us -> 57.1 us
  waiting for transfers between devices: 11.9 us -> 7.97 us
    unnamed x30 -> x50, local copies, waits for them, and re-layouts: 5.59 us -> 20.7 us
    concatenate x1 -> x0, other arithmetic: 9.48 us -> none  [per_device(): packed = jnp.concatenate([pointmaps, confidence[:, :, None, :]], 2)]
    reshape x1, local copies, waits for them, and re-layouts: 9.16 us -> 1.83 us  [per_device(): z = log_depth.reshape(img_dev, rows, LANES)]
    unnamed x1, blocking collectives: 63.5 us -> 57.1 us
    pallas_call x3, Pallas kernels: 28.4 us -> 22.1 us  [run_step(): pl.pallas_call(functools.partial(step_kernel, first), out_shape=(jax.Shap...]
    pallas_call x0 -> x1, Pallas kernels: none -> 5.36 us  [run_pack(): pl.pallas_call(pack_kernel, out_shape=(jax.ShapeDtypeStruct((pairs, high,...]
    gather x1 -> x0, local copies, waits for them, and re-layouts: 4.35 us -> none  [per_device(): send = packed[:, 1][source].reshape(blocks, slots, 4, rows, LANES)]
    all_to_all x1, waiting for transfers between devices: 11.9 us -> 7.97 us  [per_device(): far = lax.all_to_all(send, 'img', split_axis=0, concat_axis=0, tiled=True)]
  transfers between devices with their start and end apart: 1 -> 1, of which waited for: 1 -> 1; matrix products, arithmetic and copies ran while one was open for 3% -> 4% of each run, Pallas kernels for 0% -> 0%
where the time goes in v2:
time: 178 us; the launch traced here: 176 us
  Pallas kernels  69.6 us (39%)
  blocking collectives  57.1 us (32%)
  local copies, waits for them, and re-layouts  27.8 us (16%)
  waiting for transfers between devices  7.97 us (4%)
  starting transfers between devices  6.46 us (4%)
  other arithmetic  4.93 us (3%)
    unnamed x1, blocking collectives  57.1 us
    pallas_call x3, Pallas kernels, run_share(): pl.pallas_call(functools.partial(share_kernel, n_pair, n_img), out_shape=...  42.1 us
    pallas_call x3, Pallas kernels, run_step(): pl.pallas_call(functools.partial(step_kernel, first), out_shape=(jax.Shap...  22.1 us
    unnamed x50, local copies, waits for them, and re-layouts  20.7 us
    all_to_all x1, waiting for transfers between devices, per_device(): far = lax.all_to_all(send, 'img', split_axis=0, concat_axis=0, tiled=True)  7.97 us
    all_to_all x1, starting transfers between devices, per_device(): far = lax.all_to_all(send, 'img', split_axis=0, concat_axis=0, tiled=True)  6.46 us
    pallas_call x1, Pallas kernels, run_pack(): pl.pallas_call(pack_kernel, out_shape=(jax.ShapeDtypeStruct((pairs, high,...  5.36 us
  transfers between devices with their start and end apart: 1, of which 1 were waited for; matrix products, arithmetic and copies ran while one was open for 4% of the time, Pallas kernels for 0%

profile of v2, /device:TPU:0, one launch (start us, length us, event | category | flops | bytes accessed | tf_op | source)
XLA Modules:
  0.0 175.6 jit_solution(13958198222390565409)
XLA Ops:
  0.6 0.8 fusion.20
  1.5 0.2 select_reduce_fusion
  1.7 0.7 add_add_fusion.1.place
  2.4 1.7 copy-done.4
  4.1 1.1 copy-done.6
  5.2 5.4 %shard_map.85 = (bf16[16,400,128]{2,1,0:T(8,128)(2,1)S(1)}, bf16[32,400,128]{2,1,0:T(8,128)(2,1)}) custom-call(s32[16]{0:T(128)S(1)} %add_add_fusion.1.place, bf16[16,3,98,2,128]{4,3,2,1,0:T(2,128)(2,1)S(1)} %bitcast.44, bf16[16,98,2,128]{3,2,1,0:T(2,128)(2,1)S(1)} %bitcast.45), custom_call_target="tpu_custom_call" | custom-call | tf_op jit(solution)/shard_map/pallas_call | solution.py:291
  10.6 1.2 copy-done
  11.8 6.5 %all-to-all-start = ((bf16[4,8,400,128]{3,2,1,0:T(8,128)(2,1)}), bf16[4,8,400,128]{3,2,1,0:T(8,128)(2,1)S(1)}, u32[]{:S(2)}, u32[]{:S(2)}) async-start(bf16[4,8,400,128]{3,2,1,0:T(8,128)(2,1)} %bitcast.47), calls=%async_computation | async-start | bytes 6553600 | tf_op jit(solution)/shard_map/all_to_all | solution.py:428
  18.2 0.1 copy.25
  18.3 0.1 reshape.814
  18.4 0.1 copy.26
  18.5 0.1 reshape.815
  18.7 0.6 dynamic-slice
  19.9 0.2 maximum_dynamic-update-slice_fusion
  20.1 57.1 %all-reduce.1 = f32[800]{0:T(1024)S(1)} all-reduce(f32[800]{0:T(1024)S(1)} %maximum_dynamic-update-slice_fusion), channel_id=2, replica_groups=mesh['groups'=2,'img'=4,'pair'=4] {'img'}, use_global_device_ids=true, to_apply=%add.1 | all-reduce | flops 800 | bytes 6400
  77.2 0.1 reshape.835
  77.5 0.1 reshape.817
  77.6 0.1 eq.75
  77.8 0.1 reshape.818
  78.0 0.3 slice_reduce_fusion
  78.4 0.1 tile.45
  78.5 0.1 tile.47
  78.6 0.1 exp.23
  78.7 0.1 tile.37
  78.8 0.1 tile.39
  78.8 0.1 tile.41
  78.9 0.2 slice_reduce_fusion.6
  79.2 0.2 reduce_window_sum.22
  79.5 0.1 max.13
  79.6 1.8 %copy.28.z_ref = f32[8,98,128]{2,1,0:T(8,128)} copy(f32[8,98,128]{2,0,1:T(8,128)} %bitcast.50) | data formatting | bytes 802816 | tf_op jit(solution)/shard_map/reshape | solution.py:473
  81.6 0.2 fusion.12
  82.2 0.2 select_reduce_fusion.1
  82.5 0.1 fusion.2
  82.6 0.7 maximum_maximum_fusion.state
  83.2 0.7 compare_convert_fusion.same
  83.9 8.0 %all-to-all-done = bf16[4,8,400,128]{3,2,1,0:T(8,128)(2,1)S(1)} async-done(((bf16[4,8,400,128]{3,2,1,0:T(8,128)(2,1)}), bf16[4,8,400,128]{3,2,1,0:T(8,128)(2,1)S(1)}, u32[]{:S(2)}, u32[]{:S(2)}) %all-to-all-start) | async-done | bytes 3276832 | tf_op jit(solution)/shard_map/all_to_all | solution.py:428
  91.9 1.4 copy-done.1
  93.3 1.0 copy-done.5
  94.4 8.3 %shard_map.86 = (f32[8,98,128]{2,1,0:T(8,128)S(1)}, f32[40,128]{1,0:T(8,128)S(1)}) custom-call(s32[4,80]{1,0:T(4,128)S(1)} %pad_add_fusion.meta, s32[8]{0:T(128)S(1)} %broadcast_maximum_fusion.rep, f32[16,128]{1,0:T(8,128)S(1)} %concatenate.30.coef, bf16[16,400,128]{2,1,0:T(8,128)(2,1)S(1)} %copy-done.1, bf16[32,400,128]{2,1,0:T(8,128)(2,1)S(1)} %bitcast.41, ...), custom_call_target="tpu_custom_call" | custom-call | tf_op jit(solution)/shard_map/pallas_call | solution.py:310
  102.6 0.8 copy-done.9
  103.4 0.6 copy-done.14
  104.0 20.0 %shard_map.87 = (f32[16,128]{1,0:T(8,128)}, f32[16,128]{1,0:T(8,128)}) custom-call(f32[40,128]{1,0:T(8,128)} %copy-done.14, f32[16,128]{1,0:T(8,128)} %maximum_maximum_fusion.state, f32[128,128]{1,0:T(8,128)} %compare_convert_fusion.same), custom_call_target="tpu_custom_call" | custom-call | tf_op jit(solution)/shard_map/pallas_call | solution.py:384
  123.9 1.4 copy-done.2
  125.4 1.0 copy-done.10
  126.4 0.7 copy-done.15
  127.1 0.7 copy-done.18
  127.8 6.9 %shard_map.88 = (f32[8,98,128]{2,1,0:T(8,128)S(1)}, f32[40,128]{1,0:T(8,128)S(1)}) custom-call(s32[4,80]{1,0:T(4,128)S(1)} %pad_add_fusion.meta, s32[8]{0:T(128)S(1)} %broadcast_maximum_fusion.rep, f32[16,128]{1,0:T(8,128)S(1)} %copy-done.18, bf16[16,400,128]{2,1,0:T(8,128)(2,1)S(1)} %copy-done.2, bf16[32,400,128]{2,1,0:T(8,128)(2,1)S(1)} %bitcast.42, ...), custom_call_target="tpu_custom_call" | custom-call | tf_op jit(solution)/shard_map/pallas_call | solution.py:310
  134.7 0.8 copy-done.7
  135.5 0.6 copy-done.12
  136.1 10.8 %shard_map.89 = (f32[16,128]{1,0:T(8,128)}, f32[16,128]{1,0:T(8,128)}) custom-call(f32[40,128]{1,0:T(8,128)} %copy-done.12, f32[16,128]{1,0:T(8,128)} %get-tuple-element.22.state, f32[128,128]{1,0:T(8,128)} %compare_convert_fusion.same), custom_call_target="tpu_custom_call" | custom-call | tf_op jit(solution)/shard_map/pallas_call | solution.py:384
  146.9 1.4 copy-done.3
  148.3 1.0 copy-done.8
  149.3 0.7 copy-done.13
  150.1 0.7 copy-done.17
  150.8 6.9 %shard_map.90 = (f32[8,98,128]{2,1,0:T(8,128)S(1)}, f32[40,128]{1,0:T(8,128)S(1)}) custom-call(s32[4,80]{1,0:T(4,128)S(1)} %pad_add_fusion.meta, s32[8]{0:T(128)S(1)} %broadcast_maximum_fusion.rep, f32[16,128]{1,0:T(8,128)S(1)} %copy-done.17, bf16[16,400,128]{2,1,0:T(8,128)(2,1)S(1)} %copy-done.3, bf16[32,400,128]{2,1,0:T(8,128)(2,1)S(1)} %bitcast.43, ...), custom_call_target="tpu_custom_call" | custom-call | tf_op jit(solution)/shard_map/pallas_call | solution.py:310
  157.7 0.8 copy-done.11
  158.5 0.6 copy-done.16
  159.1 11.3 %shard_map.91 = (f32[16,128]{1,0:T(8,128)}, f32[16,128]{1,0:T(8,128)}) custom-call(f32[40,128]{1,0:T(8,128)} %copy-done.16, f32[16,128]{1,0:T(8,128)} %get-tuple-element.27.state, f32[128,128]{1,0:T(8,128)} %compare_convert_fusion.same), custom_call_target="tpu_custom_call" | custom-call | tf_op jit(solution)/shard_map/pallas_call | solution.py:384
  170.4 0.7 slice.115
  171.1 0.1 copy.30
  171.2 1.3 dynamic-slice_bitcast_fusion
  172.6 1.8 %copy.33 = f32[1,8,98,128]{3,1,2,0:T(8,128)} copy(f32[1,8,98,128]{3,2,1,0:T(8,128)} %bitcast.46) | data formatting | bytes 802816
  174.4 0.6 gather_fusion
  175.0 0.7 broadcast_select_fusion
  (74 shorter events, 1.5 us)
Async XLA Ops:
  2.4 1.7 copy-start.4
  4.1 1.1 copy-start.6
  10.6 1.2 copy-start
  11.7 6.5 %copy-start.21 = (s32[16,2]{0,1:T(2,128)S(1)}, s32[16,2]{0,1:T(2,128)}, u32[]{:S(2)}) copy-start(s32[16,2]{0,1:T(2,128)} %param.6) | copy-start | bytes 388
  11.7 6.7 %copy-start.20 = (f32[16,7]{0,1:T(8,128)S(1)}, f32[16,7]{0,1:T(8,128)}, u32[]{:S(2)}) copy-start(f32[16,7]{0,1:T(8,128)} %param.11) | copy-start | bytes 1348
  11.7 6.8 %copy-start.19 = (f32[8,7]{1,0:T(8,128)S(1)}, f32[8,7]{1,0:T(8,128)}, u32[]{:S(2)}) copy-start(f32[8,7]{1,0:T(8,128)} %param.10) | copy-start | bytes 676
  11.7 6.9 %copy-start.22 = (u32[32]{0:T(128)S(1)}, u32[32]{0:T(128)}, u32[]{:S(2)}) copy-start(u32[32]{0:T(128)} %constant.113) | copy-start | bytes 388
  11.8 80.2 %all-to-all-start = ((bf16[4,8,400,128]{3,2,1,0:T(8,128)(2,1)}), bf16[4,8,400,128]{3,2,1,0:T(8,128)(2,1)S(1)}, u32[]{:S(2)}, u32[]{:S(2)}) async-start(bf16[4,8,400,128]{3,2,1,0:T(8,128)(2,1)} %bitcast.47), calls=%async_computation | async-start | bytes 6553600 | tf_op jit(solution)/shard_map/all_to_all | solution.py:428
  91.9 1.4 copy-start.1
  93.3 1.0 copy-start.5
  102.6 0.8 copy-start.9
  103.4 0.6 copy-start.14
  123.9 1.4 copy-start.2
  125.4 1.0 copy-start.10
  126.4 0.7 copy-start.15
  127.1 0.7 copy-start.18
  134.7 0.8 copy-start.7
  135.5 0.6 copy-start.12
  146.9 1.4 copy-start.3
  148.3 1.0 copy-start.8
  149.3 0.7 copy-start.13
  150.1 0.7 copy-start.17
  157.7 0.8 copy-start.11
  158.4 0.6 copy-start.16

commit v3 on v2

--- a/solution.py
+++ b/solution.py
@@ -126,14 +126,17 @@
     return new
 
 
-def step_kernel(first, meta, rep, coef, own, far, z_ref, a_ref, b_ref, *rest):
-    if first:
-        z_out, mom_out, dc, total, weights = rest
+def step_kernel(mode, own_count, meta, rep, coef, z_ref, a_ref, b_ref, *rest):
+    first = mode != "all"
+    if mode == "own":
+        own, total, weights, mom_out, dc = rest
+    elif mode == "far":
+        far, total_in, weights_in, before, z_out, weights, mom_out, dc, total = rest
     else:
-        before, z_out, mom_out, dc, total, weights = rest
+        own, far, weights, before, z_out, mom_out, dc, total = rest
     images, rows, _ = z_ref.shape
     views = coef.shape[1]
-    own_count, far_count = own.shape[0], meta.shape[1] - own.shape[0]
+    far_count = meta.shape[1] - own_count
     lane = lax.broadcasted_iota(jnp.int32, (1, views), 1)
     whole = rows // CHUNK * CHUNK
     left = rows - whole
@@ -141,9 +144,17 @@
     if left:
         cuts.append(pl.ds(whole, left))
 
-    mom_out[...] = jnp.zeros_like(mom_out)
-    if not first:
-        mom_out[16:32, :] = before[16:32, :]
+    if mode == "far":
+        mom_out[...] = before[...]
+        total[...] = total_in[...]
+        weights[...] = weights_in[...]
+    else:
+        mom_out[...] = jnp.zeros_like(mom_out)
+        total[...] = jnp.zeros_like(total)
+        if mode == "own":
+            weights[...] = jnp.zeros_like(weights)
+        else:
+            mom_out[16:32, :] = before[16:32, :]
 
     def half(x):
         if x.shape[0] == 16:
@@ -179,8 +190,6 @@
             dc[g, 0, cut, :] = near * a_ref[cut, :]
             dc[g, 1, cut, :] = near * b_ref[cut, :]
             dc[g, 2, cut, :] = d
-            total[g, cut, :] = jnp.zeros((cut.size, LANES), jnp.float32)
-            weights[g, cut, :] = jnp.zeros((cut.size, LANES), jnp.float32)
         return 0
 
     lax.fori_loop(0, images, prepare, 0)
@@ -199,7 +208,8 @@
                 for k in range(3):
                     pull = pull + q[j][k] * t[j][k]
             total[g, cut, :] += pull
-            weights[g, cut, :] += w
+            if first:
+                weights[g, cut, :] += w
             new = [half(v) for v in y] + [half(t[j][k]) for j in range(3) for k in range(3)]
             sums = new if sums is None else [s + v for s, v in zip(sums, new)]
             if first:
@@ -215,7 +225,10 @@
         view(own, meta[1, i], meta[2, i], meta[3, i])
         return 0
 
-    lax.fori_loop(0, own_count, own_view, 0)
+    if mode != "far":
+        lax.fori_loop(0, own_count, own_view, 0)
+    if mode == "own":
+        return
 
     def far_view(i, _):
         at = own_count + i
@@ -297,31 +310,81 @@
         in_specs=[smem, vmem, vmem],
         out_specs=(vmem, vmem),
         scratch_shapes=[pltpu.VMEM((parts + 1, 2 * rows + 4, LANES), jnp.float32)],
-        compiler_params=pltpu.CompilerParams(vmem_limit_bytes=48 * 1024 * 1024),
+        compiler_params=pltpu.CompilerParams(vmem_limit_bytes=20 * 1024 * 1024),
     )(place, maps, conf)
 
 
-def run_step(first, meta, rep, coef, own, far, z, a, b, before):
+def run_step(mode, own_count, meta, rep, coef, z, a, b, *rest):
     images, rows, _ = z.shape
     views = coef.shape[1]
     smem = pl.BlockSpec(memory_space=pltpu.SMEM)
     vmem = pl.BlockSpec(memory_space=pltpu.VMEM)
-    args = [meta, rep, coef, own, far, z, a, b] + ([] if first else [before])
+    field = jax.ShapeDtypeStruct(z.shape, jnp.float32)
+    moments = jax.ShapeDtypeStruct((ROWS, views), jnp.float32)
+    outs = {"own": (field, field, moments), "far": (field, field, moments), "all": (field, moments)}
+    scratch = [pltpu.VMEM((images, 3, rows, LANES), jnp.float32)]
+    if mode != "own":
+        scratch.append(pltpu.VMEM((images, rows, LANES), jnp.float32))
     return pl.pallas_call(
-        functools.partial(step_kernel, first),
-        out_shape=(
-            jax.ShapeDtypeStruct(z.shape, jnp.float32),
-            jax.ShapeDtypeStruct((ROWS, views), jnp.float32),
+        functools.partial(step_kernel, mode, own_count),
+        out_shape=outs[mode],
+        in_specs=[smem] * 3 + [vmem] * (3 + len(rest)),
+        out_specs=tuple(vmem for _ in outs[mode]),
+        scratch_shapes=scratch,
+        compiler_params=pltpu.CompilerParams(vmem_limit_bytes=20 * 1024 * 1024),
+        cost_estimate=pl.CostEstimate(
+            flops=16 * 1024 * 1024 * 8, bytes_accessed=8 * 1024 * 1024, transcendentals=0
         ),
-        in_specs=[smem] * 3 + [vmem] * (len(args) - 3),
-        out_specs=(vmem, vmem),
-        scratch_shapes=[
-            pltpu.VMEM((images, 3, rows, LANES), jnp.float32),
-            pltpu.VMEM((images, rows, LANES), jnp.float32),
-            pltpu.VMEM((images, rows, LANES), jnp.float32),
-        ],
-        compiler_params=pltpu.CompilerParams(vmem_limit_bytes=32 * 1024 * 1024),
-    )(*args)
+    )(meta, rep, coef, z, a, b, *rest)
+
+
+def spread_kernel(size, small, out, send, recv):
+    me = lax.axis_index("img")
+    barrier = pltpu.get_barrier_semaphore()
+    for k in range(1, size):
+        peer = lax.rem(me + k, size)
+        pl.semaphore_signal(barrier, inc=1, device_id={"img": peer}, device_id_type=MESH)
+    pl.semaphore_wait(barrier, size - 1)
+    copies = []
+    for k in range(1, size):
+        peer = lax.rem(me + k, size)
+        copy = pltpu.make_async_remote_copy(
+            src_ref=small,
+            dst_ref=out.at[me],
+            send_sem=send.at[k],
+            recv_sem=recv.at[me],
+            device_id={"img": peer},
+            device_id_type=MESH,
+        )
+        copy.start()
+        copies.append(copy)
+    out[me] = small[...]
+    for k in range(1, size):
+        peer = lax.rem(me + k, size)
+        pltpu.make_async_remote_copy(
+            src_ref=small,
+            dst_ref=out.at[peer],
+            send_sem=send.at[k],
+            recv_sem=recv.at[peer],
+            device_id={"img": peer},
+            device_id_type=MESH,
+        ).wait_recv()
+    for copy in copies:
+        copy.wait_send()
+
+
+def run_spread(size, small):
+    vmem = pl.BlockSpec(memory_space=pltpu.VMEM)
+    return pl.pallas_call(
+        functools.partial(spread_kernel, size),
+        out_shape=jax.ShapeDtypeStruct((size,) + small.shape, jnp.float32),
+        in_specs=[vmem],
+        out_specs=vmem,
+        scratch_shapes=[pltpu.SemaphoreType.DMA((size,)), pltpu.SemaphoreType.DMA((size,))],
+        compiler_params=pltpu.CompilerParams(
+            collective_id=1, has_side_effects=True, vmem_limit_bytes=2 * 1024 * 1024
+        ),
+    )(small)
 
 
 def share_kernel(
@@ -397,7 +460,9 @@
             pltpu.SemaphoreType.DMA((n_img,)),
             pltpu.SemaphoreType.DMA((n_img,)),
         ],
-        compiler_params=pltpu.CompilerParams(collective_id=0, has_side_effects=True),
+        compiler_params=pltpu.CompilerParams(
+            collective_id=0, has_side_effects=True, vmem_limit_bytes=8 * 1024 * 1024
+        ),
     )(mom, state, same)
 
 
@@ -420,14 +485,6 @@
     hits = (target[:, None] == jnp.arange(blocks)[None, :]).astype(jnp.int32)
     rank = jnp.sum(jnp.cumsum(hits, 0) * hits, 1) - 1
     place = target * slots + rank
-    maps = pointmaps.reshape(pair_dev, 2, 3, rows, LANES).transpose(0, 2, 3, 1, 4)
-    conf = confidence.reshape(pair_dev, 2, rows, LANES).transpose(0, 2, 1, 3)
-    own, send = run_pack(place.astype(jnp.int32), blocks * slots, maps, conf)
-    high = own.shape[1]
-    send = send.reshape(blocks, slots, high, LANES)
-    far = lax.all_to_all(send, "img", split_axis=0, concat_axis=0, tiled=True)
-    far = far.reshape(blocks * slots, high, LANES)
-
     small = jnp.concatenate(
         [
             pair_images.astype(jnp.float32).reshape(-1),
@@ -435,7 +492,21 @@
             image_params.reshape(-1),
         ]
     )
-    small = lax.all_gather(small, "img")
+    count = small.shape[0]
+    tiles = -(-count // (8 * LANES))
+    small = jnp.pad(small, (0, tiles * 8 * LANES - count)).reshape(tiles * 8, LANES)
+    small = run_spread(blocks, small)
+
+    maps = pointmaps.reshape(pair_dev, 2, 3, rows, LANES).transpose(0, 2, 3, 1, 4)
+    conf = confidence.reshape(pair_dev, 2, rows, LANES).transpose(0, 2, 1, 3)
+    own, send = run_pack(place.astype(jnp.int32), blocks * slots, maps, conf)
+    high = own.shape[1]
+    small, send = lax.optimization_barrier((small, send))
+    small = small.reshape(blocks, -1)[:, :count]
+    send = send.reshape(blocks, slots, high, LANES)
+    far = lax.all_to_all(send, "img", split_axis=0, concat_axis=0, tiled=True)
+    far = far.reshape(blocks * slots, high, LANES)
+
     cut1, cut2 = 2 * pair_dev, 9 * pair_dev
     all_ids = small[:, :cut1].astype(jnp.int32).reshape(blocks * pair_dev, 2)
     all_pairs = small[:, cut1:cut2].reshape(blocks * pair_dev, 7)
@@ -471,10 +542,13 @@
     rep = jnp.maximum(rep, 0).astype(jnp.int32)
 
     z = log_depth.reshape(img_dev, rows, LANES)
-    before = None
-    for step in range(STEPS):
-        z, mom = run_step(step == 0, meta, rep, coef, own, far, z, coord_a, coord_b, before)
-        before = mom
+    head = (pair_dev, meta, rep)
+    tail = (coord_a, coord_b)
+    total, weights, mom = run_step("own", *head, coef, z, *tail, own)
+    z, weights, mom = run_step("far", *head, coef, z, *tail, far, total, weights, mom)
+    state, coef = run_share(n_pair, blocks, mom, state, same)
+    for step in range(1, STEPS):
+        z, mom = run_step("all", *head, coef, z, *tail, own, far, weights, mom)
         state, coef = run_share(n_pair, blocks, mom, state, same)
 
     new_depth = z.reshape(img_dev, pix_dev)

time: 178 us -> 155 us (0.87)
  blocking collectives: 57.1 us -> 0 us
  waiting for transfers between devices: 7.97 us -> 58.9 us
  local copies, waits for them, and re-layouts: 27.8 us -> 20.7 us
  Pallas kernels: 69.6 us -> 62.7 us
  starting transfers between devices: 6.46 us -> 4.57 us
    unnamed x1 -> x0, blocking collectives: 57.1 us -> none
    all_to_all x1, waiting for transfers between devices: 7.97 us -> 58.9 us  [per_device(): far = lax.all_to_all(send, 'img', split_axis=0, concat_axis=0, tiled=True)]
    pallas_call x3, Pallas kernels: 42.1 us -> 27.7 us  [run_share(): pl.pallas_call(functools.partial(share_kernel, n_pair, n_img), out_shape=...]
    pallas_call x3 -> x5, Pallas kernels: 22.1 us -> 31.2 us  [the longest x4 23.9 us: run_step(): pl.pallas_call(functools.partial(step_kernel, mode, own_count), out_shape...]
    unnamed x50 -> x29, local copies, waits for them, and re-layouts: 20.7 us -> 14.4 us
    all_to_all x1, starting transfers between devices: 6.46 us -> 4.57 us  [per_device(): far = lax.all_to_all(send, 'img', split_axis=0, concat_axis=0, tiled=True)]
  transfers between devices with their start and end apart: 1 -> 1, of which waited for: 1 -> 1; matrix products, arithmetic and copies ran while one was open for 4% -> 3% of each run, Pallas kernels for 0% -> 3%
where the time goes in v3:
time: 155 us; the launch traced here: 152 us
  Pallas kernels  62.7 us (40%)
  waiting for transfers between devices  58.9 us (38%)
  local copies, waits for them, and re-layouts  20.7 us (13%)
  starting transfers between devices  4.57 us (3%)
  other arithmetic  4.27 us (3%)
    all_to_all x1, waiting for transfers between devices, per_device(): far = lax.all_to_all(send, 'img', split_axis=0, concat_axis=0, tiled=True)  58.9 us
    pallas_call x3, Pallas kernels, run_share(): pl.pallas_call(functools.partial(share_kernel, n_pair, n_img), out_shape=...  27.7 us
    pallas_call x4, Pallas kernels, run_step(): pl.pallas_call(functools.partial(step_kernel, mode, own_count), out_shape...  23.9 us
    unnamed x29, local copies, waits for them, and re-layouts  14.4 us
    pallas_call x1, Pallas kernels, run_spread(): pl.pallas_call(functools.partial(spread_kernel, size), out_shape=jax.Shap...  7.32 us
    all_to_all x1, starting transfers between devices, per_device(): far = lax.all_to_all(send, 'img', split_axis=0, concat_axis=0, tiled=True)  4.57 us
    pallas_call x1, Pallas kernels, run_pack(): pl.pallas_call(pack_kernel, out_shape=(jax.ShapeDtypeStruct((pairs, high,...  3.7 us
  transfers between devices with their start and end apart: 1, of which 1 were waited for; matrix products, arithmetic and copies ran while one was open for 3% of the time, Pallas kernels for 3%

profile of v3, /device:TPU:0, one launch (start us, length us, event | category | flops | bytes accessed | tf_op | source)
XLA Modules:
  0.0 152.2 jit_solution(9756581297604915919)
XLA Ops:
  0.6 0.8 reshape.822
  1.4 0.7 convert_element_type.27
  2.1 0.8 subtract_bitcast_fusion
  2.9 0.1 copy.27
  2.9 0.1 reshape.820
  3.1 0.2 select_reduce_fusion
  3.3 0.7 add_add_fusion.3.place
  4.0 0.8 copy.28
  4.8 0.1 reshape.821
  4.9 0.1 fusion.15.small
  4.9 7.3 %shard_map.85 = f32[4,8,128]{2,1,0:T(8,128)S(1)} custom-call(f32[8,128]{1,0:T(8,128)S(1)} %fusion.15.small), custom_call_target="tpu_custom_call" | custom-call | tf_op jit(solution)/shard_map/pallas_call | solution.py:378
  12.3 1.7 %copy-done.6 = bf16[16,2,3,12544]{3,1,2,0:T(2,128)(2,1)S(1)} copy-done((bf16[16,2,3,12544]{3,1,2,0:T(2,128)(2,1)S(1)}, bf16[16,2,3,12544]{3,1,2,0:T(2,128)(2,1)}, u32[]{:S(2)}) %copy-start.6) | copy-done | bytes 2408472
  14.0 1.1 copy-done.7
  15.1 3.7 %shard_map.86 = (bf16[16,400,128]{2,1,0:T(8,128)(2,1)S(1)}, bf16[32,400,128]{2,1,0:T(8,128)(2,1)S(1)}) custom-call(s32[16]{0:T(128)S(1)} %add_add_fusion.3.place, bf16[16,3,98,2,128]{4,3,2,1,0:T(2,128)(2,1)S(1)} %bitcast.50, bf16[16,98,2,128]{3,2,1,0:T(2,128)(2,1)S(1)} %bitcast.51), custom_call_target="tpu_custom_call" | custom-call | tf_op jit(solution)/shard_map/pallas_call | solution.py:304
  18.8 1.2 copy-done
  20.0 1.7 %copy-done.5 = bf16[32,400,128]{2,1,0:T(8,128)(2,1)} copy-done((bf16[32,400,128]{2,1,0:T(8,128)(2,1)}, bf16[32,400,128]{2,1,0:T(8,128)(2,1)S(1)}, u32[]{:S(2)}) %copy-start.5) | copy-done | bytes 3276824
  21.7 4.6 %all-to-all-start = ((bf16[4,8,400,128]{3,2,1,0:T(8,128)(2,1)}), bf16[4,8,400,128]{3,2,1,0:T(8,128)(2,1)S(1)}, u32[]{:S(2)}, u32[]{:S(2)}) async-start(bf16[4,8,400,128]{3,2,1,0:T(8,128)(2,1)} %bitcast.49), calls=%async_computation | async-start | bytes 6553600 | tf_op jit(solution)/shard_map/all_to_all | solution.py:507
  26.4 1.8 %copy.31.z_ref = f32[8,98,128]{2,1,0:T(8,128)} copy(f32[8,98,128]{2,0,1:T(8,128)} %bitcast.56) | data formatting | bytes 802816 | tf_op jit(solution)/shard_map/reshape | solution.py:544
  28.2 0.1 reshape.829
  28.3 0.1 reshape.827
  28.5 0.1 eq.79
  28.6 0.2 slice_reduce_fusion.6
  28.8 0.1 reshape_squeeze.6
  28.9 0.2 reduce_window_sum.23
  29.1 0.1 add_maximum_fusion
  29.1 0.1 max.13
  29.2 0.1 reshape.828
  29.4 0.3 slice_reduce_fusion
  29.7 0.1 tile.47
  29.8 0.1 tile.45
  29.9 0.1 tile.43
  30.0 0.1 tile.41
  30.1 0.1 tile.39
  30.2 0.1 tile.37
  30.2 0.1 exp.23
  30.3 0.1 tile.49
  30.4 0.1 pad.9.clone
  30.5 0.2 fusion.12
  30.9 0.1 fusion.20
  31.0 0.1 add_bitcast_fusion.2
  31.1 0.1 add_bitcast_fusion
  31.2 0.2 select_reduce_fusion.1
  31.4 0.1 fusion.2
  31.5 1.4 copy-done.1
  32.9 1.0 copy-done.3
  33.9 4.1 %shard_map.87 = (f32[8,98,128]{2,1,0:T(8,128)S(1)}, f32[8,98,128]{2,1,0:T(8,128)S(1)}, f32[40,128]{1,0:T(8,128)S(1)}) custom-call(s32[4,80]{1,0:T(4,128)S(1)} %pad_add_fusion.meta, s32[8]{0:T(128)S(1)} %broadcast_maximum_fusion.rep, f32[16,128]{1,0:T(8,128)S(1)} %concatenate.30.coef, f32[8,98,128]{2,1,0:T(8,128)S(1)} %copy-done.3, ...), custom_call_target="tpu_custom_call" | custom-call | flops 134217728 | bytes 8388608 | tf_op jit(solution)/shard_map/pallas_call | solution.py:328
  38.0 0.8 copy-done.8
  38.7 0.8 copy-done.10
  39.6 0.1 compare_convert_fusion.same
  39.7 58.9 %all-to-all-done = bf16[4,8,400,128]{3,2,1,0:T(8,128)(2,1)S(1)} async-done(((bf16[4,8,400,128]{3,2,1,0:T(8,128)(2,1)}), bf16[4,8,400,128]{3,2,1,0:T(8,128)(2,1)S(1)}, u32[]{:S(2)}, u32[]{:S(2)}) %all-to-all-start) | async-done | bytes 3276832 | tf_op jit(solution)/shard_map/all_to_all | solution.py:507
  98.6 1.1 copy-done.4
  99.7 1.0 copy-done.9
  100.7 1.0 copy-done.11
  101.7 5.5 %shard_map.88 = (f32[8,98,128]{2,1,0:T(8,128)S(1)}, f32[8,98,128]{2,1,0:T(8,128)S(1)}, f32[40,128]{1,0:T(8,128)S(1)}) custom-call(s32[4,80]{1,0:T(4,128)S(1)} %pad_add_fusion.meta, s32[8]{0:T(128)S(1)} %broadcast_maximum_fusion.rep, f32[16,128]{1,0:T(8,128)S(1)} %concatenate.30.coef, f32[8,98,128]{2,1,0:T(8,128)S(1)} %copy-done.4, ...), custom_call_target="tpu_custom_call" | custom-call | flops 134217728 | bytes 8388608 | tf_op jit(solution)/shard_map/pallas_call | solution.py:328
  107.2 9.4 %shard_map.89 = (f32[16,128]{1,0:T(8,128)S(1)}, f32[16,128]{1,0:T(8,128)S(1)}) custom-call(f32[40,128]{1,0:T(8,128)S(1)} %get-tuple-element.29.mom.rest_3_, f32[16,128]{1,0:T(8,128)S(1)} %maximum_maximum_fusion.state, f32[128,128]{1,0:T(8,128)S(1)} %compare_convert_fusion.same), custom_call_target="tpu_custom_call" | custom-call | tf_op jit(solution)/shard_map/pallas_call | solution.py:447
  116.6 7.2 %shard_map.90 = (f32[8,98,128]{2,1,0:T(8,128)S(1)}, f32[40,128]{1,0:T(8,128)S(1)}) custom-call(s32[4,80]{1,0:T(4,128)S(1)} %pad_add_fusion.meta, s32[8]{0:T(128)S(1)} %broadcast_maximum_fusion.rep, f32[16,128]{1,0:T(8,128)S(1)} %get-tuple-element.30.coef, f32[8,98,128]{2,1,0:T(8,128)S(1)} %get-tuple-element.31.z_ref, f32[98,128]{1,0:T(8,128)S(1)} %get-tuple-element.95.a_ref, ...), custom_call_target="tpu_custom_call" | custom-call | flops 134217728 | bytes 8388608 | tf_op jit(solution)/shard_map/pallas_call | solution.py:328
  123.8 8.4 %shard_map.91 = (f32[16,128]{1,0:T(8,128)S(1)}, f32[16,128]{1,0:T(8,128)S(1)}) custom-call(f32[40,128]{1,0:T(8,128)S(1)} %get-tuple-element.33.mom.rest_3_, f32[16,128]{1,0:T(8,128)S(1)} %get-tuple-element.34.state, f32[128,128]{1,0:T(8,128)S(1)} %compare_convert_fusion.same), custom_call_target="tpu_custom_call" | custom-call | tf_op jit(solution)/shard_map/pallas_call | solution.py:447
  132.2 7.2 %shard_map.92 = (f32[8,98,128]{2,1,0:T(8,128)S(1)}, f32[40,128]{1,0:T(8,128)S(1)}) custom-call(s32[4,80]{1,0:T(4,128)S(1)} %pad_add_fusion.meta, s32[8]{0:T(128)S(1)} %broadcast_maximum_fusion.rep, f32[16,128]{1,0:T(8,128)S(1)} %get-tuple-element.35.coef, f32[8,98,128]{2,1,0:T(8,128)S(1)} %get-tuple-element.36.z_ref, f32[98,128]{1,0:T(8,128)S(1)} %get-tuple-element.95.a_ref, ...), custom_call_target="tpu_custom_call" | custom-call | flops 134217728 | bytes 8388608 | tf_op jit(solution)/shard_map/pallas_call | solution.py:328
  139.4 0.8 copy.38
  140.2 9.9 %shard_map.93 = (f32[16,128]{1,0:T(8,128)S(1)}, f32[16,128]{1,0:T(8,128)}) custom-call(f32[40,128]{1,0:T(8,128)S(1)} %get-tuple-element.38.mom, f32[16,128]{1,0:T(8,128)S(1)} %get-tuple-element.39.state, f32[128,128]{1,0:T(8,128)S(1)} %compare_convert_fusion.same), custom_call_target="tpu_custom_call" | custom-call | tf_op jit(solution)/shard_map/pallas_call | solution.py:447
  150.1 0.7 dynamic-slice_bitcast_fusion
  150.8 0.1 copy.33
  150.9 0.6 gather_fusion
  151.5 0.7 broadcast_select_fusion
  (53 shorter events, 0.8 us)
Async XLA Ops:
  12.3 1.7 %copy-start.6 = (bf16[16,2,3,12544]{3,1,2,0:T(2,128)(2,1)S(1)}, bf16[16,2,3,12544]{3,1,2,0:T(2,128)(2,1)}, u32[]{:S(2)}) copy-start(bf16[16,2,3,12544]{3,1,2,0:T(2,128)(2,1)} %param.7) | copy-start | bytes 7225348
  14.0 1.1 copy-start.7
  18.8 1.2 copy-start
  20.0 1.7 %copy-start.5 = (bf16[32,400,128]{2,1,0:T(8,128)(2,1)}, bf16[32,400,128]{2,1,0:T(8,128)(2,1)S(1)}, u32[]{:S(2)}) copy-start(bf16[32,400,128]{2,1,0:T(8,128)(2,1)S(1)} %get-tuple-element.24) | copy-start | bytes 9830404
  21.7 76.9 %all-to-all-start = ((bf16[4,8,400,128]{3,2,1,0:T(8,128)(2,1)}), bf16[4,8,400,128]{3,2,1,0:T(8,128)(2,1)S(1)}, u32[]{:S(2)}, u32[]{:S(2)}) async-start(bf16[4,8,400,128]{3,2,1,0:T(8,128)(2,1)} %bitcast.49), calls=%async_computation | async-start | bytes 6553600 | tf_op jit(solution)/shard_map/all_to_all | solution.py:507
  31.5 1.4 copy-start.1
  32.9 1.0 copy-start.3
  38.0 0.8 copy-start.8
  38.7 0.8 copy-start.10
  98.6 18.1 %copy-start.2 = (bf16[16,400,128]{2,1,0:T(8,128)(2,1)S(1)}, bf16[16,400,128]{2,1,0:T(8,128)(2,1)}, u32[]{:S(2)}) copy-start(bf16[16,400,128]{2,1,0:T(8,128)(2,1)} %copy-done) | copy-start | bytes 4915204
  98.6 1.1 copy-start.4
  99.7 1.0 copy-start.9
  100.7 1.0 copy-start.11
  132.2 19.3 %copy-start.12 = (f32[8,7]{1,0:T(8,128)S(1)}, f32[8,7]{1,0:T(8,128)}, u32[]{:S(2)}) copy-start(f32[8,7]{1,0:T(8,128)} %param.10) | copy-start | bytes 676

commit v4 on v3

--- a/solution.py
+++ b/solution.py
@@ -258,38 +258,27 @@
 
 
 def pack_kernel(place, maps, conf, own, send, wide):
-    pairs, parts, rows, _, _ = maps.shape
+    _, parts, rows, _, _ = maps.shape
     whole = rows // CHUNK * CHUNK
     left = rows - whole
-
-    def pair(i, _):
-        tails = [[], []]
-        for k in range(parts + 1):
-            both = maps[i, k] if k < parts else conf[i]
-            wide[k, 0 : 2 * rows, :] = both.astype(jnp.float32).reshape(2 * rows, LANES)
-            for v in range(2):
-                body = wide[k, pl.ds(v, whole, stride=2), :].astype(jnp.bfloat16)
-                if v == 0:
-                    own[i, k * whole : (k + 1) * whole, :] = body
-                else:
-                    send[place[i], k * whole : (k + 1) * whole, :] = body
-                if left:
-                    tails[v].append(wide[k, pl.ds(2 * whole + v, left, stride=2), :])
-        if left:
-            start = (parts + 1) * whole
-            spare = tail_rows(rows) - (parts + 1) * left
-            for v in range(2):
-                lines = tails[v]
-                if spare:
-                    lines = lines + [jnp.zeros((spare, LANES), jnp.float32)]
-                tail = jnp.concatenate(lines, 0).astype(jnp.bfloat16)
-                if v == 0:
-                    own[i, start:, :] = tail
-                else:
-                    send[place[i], start:, :] = tail
-        return 0
-
-    lax.fori_loop(0, pairs, pair, 0)
+    tails = [[], []]
+    outs = (own, send)
+    for k in range(parts + 1):
+        both = maps[0, k] if k < parts else conf[0]
+        wide[k, 0 : 2 * rows, :] = both.astype(jnp.float32).reshape(2 * rows, LANES)
+        for v in range(2):
+            body = wide[k, pl.ds(v, whole, stride=2), :].astype(jnp.bfloat16)
+            outs[v][0, k * whole : (k + 1) * whole, :] = body
+            if left:
+                tails[v].append(wide[k, pl.ds(2 * whole + v, left, stride=2), :])
+    if left:
+        start = (parts + 1) * whole
+        spare = tail_rows(rows) - (parts + 1) * left
+        for v in range(2):
+            lines = tails[v]
+            if spare:
+                lines = lines + [jnp.zeros((spare, LANES), jnp.float32)]
+            outs[v][0, start:, :] = jnp.concatenate(lines, 0).astype(jnp.bfloat16)
 
 
 def tail_rows(rows):
@@ -299,18 +288,26 @@
 def run_pack(place, slots, maps, conf):
     pairs, parts, rows, _, _ = maps.shape
     high = (parts + 1) * (rows // CHUNK * CHUNK) + tail_rows(rows)
-    smem = pl.BlockSpec(memory_space=pltpu.SMEM)
-    vmem = pl.BlockSpec(memory_space=pltpu.VMEM)
     return pl.pallas_call(
         pack_kernel,
         out_shape=(
             jax.ShapeDtypeStruct((pairs, high, LANES), jnp.bfloat16),
             jax.ShapeDtypeStruct((slots, high, LANES), jnp.bfloat16),
         ),
-        in_specs=[smem, vmem, vmem],
-        out_specs=(vmem, vmem),
-        scratch_shapes=[pltpu.VMEM((parts + 1, 2 * rows + 4, LANES), jnp.float32)],
-        compiler_params=pltpu.CompilerParams(vmem_limit_bytes=20 * 1024 * 1024),
+        grid_spec=pltpu.PrefetchScalarGridSpec(
+            num_scalar_prefetch=1,
+            grid=(pairs,),
+            in_specs=[
+                pl.BlockSpec((1, parts, rows, 2, LANES), lambda i, at: (i, 0, 0, 0, 0)),
+                pl.BlockSpec((1, rows, 2, LANES), lambda i, at: (i, 0, 0, 0)),
+            ],
+            out_specs=[
+                pl.BlockSpec((1, high, LANES), lambda i, at: (i, 0, 0)),
+                pl.BlockSpec((1, high, LANES), lambda i, at: (at[i], 0, 0)),
+            ],
+            scratch_shapes=[pltpu.VMEM((parts + 1, 2 * rows + 4, LANES), jnp.float32)],
+        ),
+        compiler_params=pltpu.CompilerParams(vmem_limit_bytes=60 * 1024 * 1024),
     )(place, maps, conf)
 
 
@@ -495,13 +492,13 @@
     count = small.shape[0]
     tiles = -(-count // (8 * LANES))
     small = jnp.pad(small, (0, tiles * 8 * LANES - count)).reshape(tiles * 8, LANES)
-    small = run_spread(blocks, small)
 
     maps = pointmaps.reshape(pair_dev, 2, 3, rows, LANES).transpose(0, 2, 3, 1, 4)
     conf = confidence.reshape(pair_dev, 2, rows, LANES).transpose(0, 2, 1, 3)
     own, send = run_pack(place.astype(jnp.int32), blocks * slots, maps, conf)
     high = own.shape[1]
     small, send = lax.optimization_barrier((small, send))
+    small = run_spread(blocks, small)
     small = small.reshape(blocks, -1)[:, :count]
     send = send.reshape(blocks, slots, high, LANES)
     far = lax.all_to_all(send, "img", split_axis=0, concat_axis=0, tiled=True)

time: 155 us -> 168 us (1.084); the launches traced: 152 us -> 169 us
  Pallas kernels: 62.7 us -> 141 us
  waiting for transfers between devices: 58.9 us -> 0.01 us
  local copies, waits for them, and re-layouts: 20.7 us -> 15 us
  starting transfers between devices: 4.57 us -> 6.31 us
    pallas_call x1, Pallas kernels: 7.32 us -> 73.9 us  [run_spread(): pl.pallas_call(functools.partial(spread_kernel, size), out_shape=jax.Shap...]
    all_to_all x1, waiting for transfers between devices: 58.9 us -> 0.01 us  [per_device(): far = lax.all_to_all(send, 'img', split_axis=0, concat_axis=0, tiled=True)]
    pallas_call x1, Pallas kernels: 3.7 us -> 11.6 us  [run_pack(): pl.pallas_call(pack_kernel, out_shape=(jax.ShapeDtypeStruct((pairs, high,...]
    unnamed x29 -> x21, local copies, waits for them, and re-layouts: 14.4 us -> 8.69 us
    pallas_call x4, Pallas kernels: 23.9 us -> 28.3 us  [run_step(): pl.pallas_call(functools.partial(step_kernel, mode, own_count), out_shape...]
    all_to_all x1, starting transfers between devices: 4.57 us -> 6.31 us  [per_device(): far = lax.all_to_all(send, 'img', split_axis=0, concat_axis=0, tiled=True)]
  transfers between devices with their start and end apart: 1 -> 1, of which waited for: 1 -> 0; matrix products, arithmetic and copies ran while one was open for 3% -> 3% of each run, Pallas kernels for 3% -> 46%
where the time goes in v4:
time: 168 us; the launch traced here: 169 us
  Pallas kernels  141 us (84%)
  local copies, waits for them, and re-layouts  15 us (9%)
  starting transfers between devices  6.31 us (4%)
  other arithmetic  4.78 us (3%)
    pallas_call x1, Pallas kernels, run_spread(): pl.pallas_call(functools.partial(spread_kernel, size), out_shape=jax.Shap...  73.9 us
    pallas_call x4, Pallas kernels, run_step(): pl.pallas_call(functools.partial(step_kernel, mode, own_count), out_shape...  28.3 us
    pallas_call x3, Pallas kernels, run_share(): pl.pallas_call(functools.partial(share_kernel, n_pair, n_img), out_shape=...  27.7 us
    pallas_call x1, Pallas kernels, run_pack(): pl.pallas_call(pack_kernel, out_shape=(jax.ShapeDtypeStruct((pairs, high,...  11.6 us
    unnamed x21, local copies, waits for them, and re-layouts  8.69 us
    all_to_all x1, starting transfers between devices, per_device(): far = lax.all_to_all(send, 'img', split_axis=0, concat_axis=0, tiled=True)  6.31 us
  transfers between devices with their start and end apart: 1, of which 0 were waited for; matrix products, arithmetic and copies ran while one was open for 3% of the time, Pallas kernels for 46%

profile of v4, /device:TPU:0, one launch (start us, length us, event | category | flops | bytes accessed | tf_op | source)
XLA Modules:
  0.0 168.7 jit_solution(8857915779150264888)
XLA Ops:
  0.6 0.8 reshape.822
  1.4 0.7 convert_element_type.27
  2.1 0.8 subtract_bitcast_fusion
  2.9 0.1 copy.27
  2.9 0.1 reshape.820
  3.0 0.1 fusion.14
  3.1 0.2 select_reduce_fusion
  3.3 1.2 add_add_fusion.3.place
  4.5 0.8 copy.28
  5.3 0.1 reshape.821
  5.4 0.1 fusion.15.small
  5.5 11.6 %shard_map.85 = (bf16[16,400,128]{2,1,0:T(8,128)(2,1)}, bf16[32,400,128]{2,1,0:T(8,128)(2,1)}) custom-call(s32[16]{0:T(128)} %add_add_fusion.3.place, bf16[16,3,98,2,128]{4,3,2,1,0:T(2,128)(2,1)} %bitcast.54, bf16[16,98,2,128]{3,2,1,0:T(2,128)(2,1)} %bitcast.55), custom_call_target="tpu_custom_call" | custom-call | tf_op jit(solution)/shard_map/pallas_call | solution.py:291
  17.0 6.3 %all-to-all-start = ((bf16[4,8,400,128]{3,2,1,0:T(8,128)(2,1)}), bf16[4,8,400,128]{3,2,1,0:T(8,128)(2,1)S(1)}, u32[]{:S(2)}, u32[]{:S(2)}) async-start(bf16[4,8,400,128]{3,2,1,0:T(8,128)(2,1)} %bitcast.51), calls=%async_computation | async-start | bytes 6553600 | tf_op jit(solution)/shard_map/all_to_all | solution.py:504
  23.4 73.9 %shard_map.86 = f32[4,8,128]{2,1,0:T(8,128)S(1)} custom-call(f32[8,128]{1,0:T(8,128)S(1)} %fusion.15.small), custom_call_target="tpu_custom_call" | custom-call | tf_op jit(solution)/shard_map/pallas_call | solution.py:375
  97.2 0.1 slice.126
  97.3 0.1 slice.124
  97.4 1.8 %copy.31.z_ref = f32[8,98,128]{2,1,0:T(8,128)} copy(f32[8,98,128]{2,0,1:T(8,128)} %bitcast.56) | data formatting | bytes 802816 | tf_op jit(solution)/shard_map/reshape | solution.py:541
  99.2 0.1 reshape.829
  99.3 0.1 reshape.827
  99.4 0.1 copy.29
  99.5 0.1 eq.79
  99.6 0.2 slice_reduce_fusion.6
  99.8 0.1 reshape_squeeze.6
  99.9 0.2 reduce_window_sum.23
  100.1 0.1 add_maximum_fusion
  100.1 0.1 max.13
  100.2 0.1 reshape.828
  100.4 0.3 slice_reduce_fusion
  100.7 0.1 tile.47
  100.8 0.1 tile.45
  100.9 0.1 tile.43
  101.0 0.1 tile.41
  101.1 0.1 tile.39
  101.2 0.1 tile.37
  101.2 0.1 exp.23
  101.3 0.1 tile.49
  101.4 0.1 pad.9.clone
  101.5 0.2 fusion.12
  101.9 0.1 fusion.20
  102.0 0.1 add_bitcast_fusion.2
  102.1 0.1 add_bitcast_fusion
  102.2 0.2 select_reduce_fusion.1
  102.4 0.1 fusion.2
  102.5 1.4 copy-done
  103.9 1.0 copy-done.2
  104.9 4.1 %shard_map.87 = (f32[8,98,128]{2,1,0:T(8,128)S(1)}, f32[8,98,128]{2,1,0:T(8,128)S(1)}, f32[40,128]{1,0:T(8,128)S(1)}) custom-call(s32[4,80]{1,0:T(4,128)S(1)} %pad_add_fusion.meta, s32[8]{0:T(128)S(1)} %broadcast_maximum_fusion.rep, f32[16,128]{1,0:T(8,128)S(1)} %concatenate.30.coef, f32[8,98,128]{2,1,0:T(8,128)S(1)} %copy-done.2, ...), custom_call_target="tpu_custom_call" | custom-call | flops 134217728 | bytes 8388608 | tf_op jit(solution)/shard_map/pallas_call | solution.py:325
  109.0 0.8 copy-done.4
  109.8 0.8 copy-done.6
  110.5 0.1 maximum_maximum_fusion.state
  110.6 0.1 compare_convert_fusion.same
  110.7 1.1 copy-done.3
  111.8 1.0 copy-done.5
  112.8 1.0 copy-done.7
  113.8 7.3 %shard_map.88 = (f32[8,98,128]{2,1,0:T(8,128)S(1)}, f32[8,98,128]{2,1,0:T(8,128)S(1)}, f32[40,128]{1,0:T(8,128)S(1)}) custom-call(s32[4,80]{1,0:T(4,128)S(1)} %pad_add_fusion.meta, s32[8]{0:T(128)S(1)} %broadcast_maximum_fusion.rep, f32[16,128]{1,0:T(8,128)S(1)} %concatenate.30.coef, f32[8,98,128]{2,1,0:T(8,128)S(1)} %copy-done.3, ...), custom_call_target="tpu_custom_call" | custom-call | flops 134217728 | bytes 8388608 | tf_op jit(solution)/shard_map/pallas_call | solution.py:325
  121.2 9.4 %shard_map.89 = (f32[16,128]{1,0:T(8,128)S(1)}, f32[16,128]{1,0:T(8,128)S(1)}) custom-call(f32[40,128]{1,0:T(8,128)S(1)} %get-tuple-element.29.mom.rest_3_, f32[16,128]{1,0:T(8,128)S(1)} %maximum_maximum_fusion.state, f32[128,128]{1,0:T(8,128)S(1)} %compare_convert_fusion.same), custom_call_target="tpu_custom_call" | custom-call | tf_op jit(solution)/shard_map/pallas_call | solution.py:444
  130.5 8.5 %shard_map.90 = (f32[8,98,128]{2,1,0:T(8,128)S(1)}, f32[40,128]{1,0:T(8,128)S(1)}) custom-call(s32[4,80]{1,0:T(4,128)S(1)} %pad_add_fusion.meta, s32[8]{0:T(128)S(1)} %broadcast_maximum_fusion.rep, f32[16,128]{1,0:T(8,128)S(1)} %get-tuple-element.30.coef, f32[8,98,128]{2,1,0:T(8,128)S(1)} %get-tuple-element.31.z_ref, f32[98,128]{1,0:T(8,128)S(1)} %get-tuple-element.95.a_ref, ...), custom_call_target="tpu_custom_call" | custom-call | flops 134217728 | bytes 8388608 | tf_op jit(solution)/shard_map/pallas_call | solution.py:325
  139.0 8.4 %shard_map.91 = (f32[16,128]{1,0:T(8,128)S(1)}, f32[16,128]{1,0:T(8,128)S(1)}) custom-call(f32[40,128]{1,0:T(8,128)S(1)} %get-tuple-element.33.mom.rest_3_, f32[16,128]{1,0:T(8,128)S(1)} %get-tuple-element.34.state, f32[128,128]{1,0:T(8,128)S(1)} %compare_convert_fusion.same), custom_call_target="tpu_custom_call" | custom-call | tf_op jit(solution)/shard_map/pallas_call | solution.py:444
  147.4 8.5 %shard_map.92 = (f32[8,98,128]{2,1,0:T(8,128)S(1)}, f32[40,128]{1,0:T(8,128)S(1)}) custom-call(s32[4,80]{1,0:T(4,128)S(1)} %pad_add_fusion.meta, s32[8]{0:T(128)S(1)} %broadcast_maximum_fusion.rep, f32[16,128]{1,0:T(8,128)S(1)} %get-tuple-element.35.coef, f32[8,98,128]{2,1,0:T(8,128)S(1)} %get-tuple-element.36.z_ref, f32[98,128]{1,0:T(8,128)S(1)} %get-tuple-element.95.a_ref, ...), custom_call_target="tpu_custom_call" | custom-call | flops 134217728 | bytes 8388608 | tf_op jit(solution)/shard_map/pallas_call | solution.py:325
  155.9 0.8 copy.38
  156.7 9.9 %shard_map.93 = (f32[16,128]{1,0:T(8,128)S(1)}, f32[16,128]{1,0:T(8,128)}) custom-call(f32[40,128]{1,0:T(8,128)S(1)} %get-tuple-element.38.mom, f32[16,128]{1,0:T(8,128)S(1)} %get-tuple-element.39.state, f32[128,128]{1,0:T(8,128)S(1)} %compare_convert_fusion.same), custom_call_target="tpu_custom_call" | custom-call | tf_op jit(solution)/shard_map/pallas_call | solution.py:444
  166.7 0.7 dynamic-slice_bitcast_fusion
  167.3 0.1 copy.33
  167.4 0.6 gather_fusion
  168.0 0.7 broadcast_select_fusion
  (45 shorter events, 0.4 us)
Async XLA Ops:
  17.0 93.6 %all-to-all-start = ((bf16[4,8,400,128]{3,2,1,0:T(8,128)(2,1)}), bf16[4,8,400,128]{3,2,1,0:T(8,128)(2,1)S(1)}, u32[]{:S(2)}, u32[]{:S(2)}) async-start(bf16[4,8,400,128]{3,2,1,0:T(8,128)(2,1)} %bitcast.51), calls=%async_computation | async-start | bytes 6553600 | tf_op jit(solution)/shard_map/all_to_all | solution.py:504
  102.5 1.4 copy-start
  103.9 1.0 copy-start.2
  109.0 0.8 copy-start.4
  109.7 0.8 copy-start.6
  110.7 19.8 %copy-start.1 = (bf16[16,400,128]{2,1,0:T(8,128)(2,1)S(1)}, bf16[16,400,128]{2,1,0:T(8,128)(2,1)}, u32[]{:S(2)}) copy-start(bf16[16,400,128]{2,1,0:T(8,128)(2,1)} %get-tuple-element.25.rest_0_) | copy-start | bytes 4915204
  110.7 1.1 copy-start.3
  111.8 1.0 copy-start.5
  112.8 1.0 copy-start.7
  147.4 20.6 %copy-start.8 = (f32[8,7]{1,0:T(8,128)S(1)}, f32[8,7]{1,0:T(8,128)}, u32[]{:S(2)}) copy-start(f32[8,7]{1,0:T(8,128)} %param.10) | copy-start | bytes 676

commit v5 on v3

--- a/solution.py
+++ b/solution.py
@@ -226,7 +226,7 @@
         return 0
 
     if mode != "far":
-        lax.fori_loop(0, own_count, own_view, 0)
+        lax.fori_loop(0, own_count, own_view, 0, unroll=2)
     if mode == "own":
         return
 
@@ -485,16 +485,10 @@
     hits = (target[:, None] == jnp.arange(blocks)[None, :]).astype(jnp.int32)
     rank = jnp.sum(jnp.cumsum(hits, 0) * hits, 1) - 1
     place = target * slots + rank
-    small = jnp.concatenate(
-        [
-            pair_images.astype(jnp.float32).reshape(-1),
-            pair_params.reshape(-1),
-            image_params.reshape(-1),
-        ]
-    )
-    count = small.shape[0]
-    tiles = -(-count // (8 * LANES))
-    small = jnp.pad(small, (0, tiles * 8 * LANES - count)).reshape(tiles * 8, LANES)
+    ids = jnp.pad(pair_images.astype(jnp.float32), ((0, img_dev), (0, LANES - 2)))
+    poses = jnp.pad(pair_params, ((0, img_dev), (2, LANES - 9)))
+    cameras = jnp.pad(image_params, ((pair_dev, 0), (2, LANES - 9)))
+    small = ids + poses + cameras
     small = run_spread(blocks, small)
 
     maps = pointmaps.reshape(pair_dev, 2, 3, rows, LANES).transpose(0, 2, 3, 1, 4)
@@ -502,15 +496,13 @@
     own, send = run_pack(place.astype(jnp.int32), blocks * slots, maps, conf)
     high = own.shape[1]
     small, send = lax.optimization_barrier((small, send))
-    small = small.reshape(blocks, -1)[:, :count]
     send = send.reshape(blocks, slots, high, LANES)
     far = lax.all_to_all(send, "img", split_axis=0, concat_axis=0, tiled=True)
     far = far.reshape(blocks * slots, high, LANES)
 
-    cut1, cut2 = 2 * pair_dev, 9 * pair_dev
-    all_ids = small[:, :cut1].astype(jnp.int32).reshape(blocks * pair_dev, 2)
-    all_pairs = small[:, cut1:cut2].reshape(blocks * pair_dev, 7)
-    all_images = small[:, cut2:].reshape(blocks * img_dev, 7)
+    all_ids = small[:, :pair_dev, :2].astype(jnp.int32).reshape(blocks * pair_dev, 2)
+    all_pairs = small[:, :pair_dev, 2:9].reshape(blocks * pair_dev, 7)
+    all_images = small[:, pair_dev:, 2:9].reshape(blocks * img_dev, 7)
     image_of = all_ids.T.reshape(-1)
     views = image_of.shape[0]
     pairs = views // 2

time: 155 us -> 152 us (0.981); the launches traced: 152 us -> 152 us
  local copies, waits for them, and re-layouts: 20.7 us -> 19 us
    unnamed x29 -> x28, local copies, waits for them, and re-layouts: 14.4 us -> 14.4 us
  transfers between devices with their start and end apart: 1 -> 1, of which waited for: 1 -> 1; matrix products, arithmetic and copies ran while one was open for 3% -> 3% of each run, Pallas kernels for 3% -> 2%
where the time goes in v5:
time: 152 us
  Pallas kernels  62.2 us (41%)
  waiting for transfers between devices  60.1 us (40%)
  local copies, waits for them, and re-layouts  19 us (12%)
  other arithmetic  4.95 us (3%)
  starting transfers between devices  4.64 us (3%)
    all_to_all x1, waiting for transfers between devices, per_device(): far = lax.all_to_all(send, 'img', split_axis=0, concat_axis=0, tiled=True)  60.1 us
    pallas_call x3, Pallas kernels, run_share(): pl.pallas_call(functools.partial(share_kernel, n_pair, n_img), out_shape=...  28.6 us
    pallas_call x4, Pallas kernels, run_step(): pl.pallas_call(functools.partial(step_kernel, mode, own_count), out_shape...  22.4 us
    unnamed x28, local copies, waits for them, and re-layouts  14.4 us
    pallas_call x1, Pallas kernels, run_spread(): pl.pallas_call(functools.partial(spread_kernel, size), out_shape=jax.Shap...  7.51 us
    all_to_all x1, starting transfers between devices, per_device(): far = lax.all_to_all(send, 'img', split_axis=0, concat_axis=0, tiled=True)  4.64 us
    pallas_call x1, Pallas kernels, run_pack(): pl.pallas_call(pack_kernel, out_shape=(jax.ShapeDtypeStruct((pairs, high,...  3.7 us
  transfers between devices with their start and end apart: 1, of which 1 were waited for; matrix products, arithmetic and copies ran while one was open for 3% of the time, Pallas kernels for 2%

profile of v5, /device:TPU:0, one launch (start us, length us, event | category | flops | bytes accessed | tf_op | source)
XLA Modules:
  0.0 152.0 jit_solution(8158591747836308544)
XLA Ops:
  0.6 0.8 copy.29
  1.4 0.7 convert_element_type.31
  2.1 0.1 copy.28
  2.2 0.8 pad_add_fusion.small
  2.9 7.5 %shard_map.85 = f32[4,24,128]{2,1,0:T(8,128)S(1)} custom-call(f32[24,128]{1,0:T(8,128)S(1)} %pad_add_fusion.small), custom_call_target="tpu_custom_call" | custom-call | tf_op jit(solution)/shard_map/pallas_call | solution.py:378
  10.4 0.8 subtract_bitcast_fusion
  11.2 0.1 fusion.15
  11.3 0.2 select_reduce_fusion
  11.5 0.7 add_add_fusion.3.place
  12.2 1.7 %copy-done.6 = bf16[16,2,3,12544]{3,1,2,0:T(2,128)(2,1)S(1)} copy-done((bf16[16,2,3,12544]{3,1,2,0:T(2,128)(2,1)S(1)}, bf16[16,2,3,12544]{3,1,2,0:T(2,128)(2,1)}, u32[]{:S(2)}) %copy-start.6) | copy-done | bytes 2408472
  13.9 1.1 copy-done.7
  15.0 3.7 %shard_map.86 = (bf16[16,400,128]{2,1,0:T(8,128)(2,1)S(1)}, bf16[32,400,128]{2,1,0:T(8,128)(2,1)S(1)}) custom-call(s32[16]{0:T(128)S(1)} %add_add_fusion.3.place, bf16[16,3,98,2,128]{4,3,2,1,0:T(2,128)(2,1)S(1)} %bitcast.76, bf16[16,98,2,128]{3,2,1,0:T(2,128)(2,1)S(1)} %bitcast.77), custom_call_target="tpu_custom_call" | custom-call | tf_op jit(solution)/shard_map/pallas_call | solution.py:304
  18.7 0.0 copy-start
  18.7 1.2 copy-done
  19.9 1.7 %copy-done.5 = bf16[32,400,128]{2,1,0:T(8,128)(2,1)} copy-done((bf16[32,400,128]{2,1,0:T(8,128)(2,1)}, bf16[32,400,128]{2,1,0:T(8,128)(2,1)S(1)}, u32[]{:S(2)}) %copy-start.5) | copy-done | bytes 3276824
  21.6 4.6 %all-to-all-start = ((bf16[4,8,400,128]{3,2,1,0:T(8,128)(2,1)}), bf16[4,8,400,128]{3,2,1,0:T(8,128)(2,1)S(1)}, u32[]{:S(2)}, u32[]{:S(2)}) async-start(bf16[4,8,400,128]{3,2,1,0:T(8,128)(2,1)} %bitcast.75), calls=%async_computation | async-start | bytes 6553600 | tf_op jit(solution)/shard_map/all_to_all | solution.py:500
  26.2 0.1 slice.93
  26.3 0.1 copy.35
  26.4 0.1 reshape_squeeze.6
  26.5 0.2 reduce_window_sum.23
  26.7 0.1 add_maximum_fusion
  26.8 0.1 max.13
  26.9 0.1 eq.79
  27.0 0.1 copy.31
  27.1 0.1 exp.23
  27.1 0.1 tile.43
  27.2 0.1 tile.45
  27.3 0.1 tile.47
  27.4 0.1 tile.39
  27.5 0.1 tile.41
  27.6 0.1 tile.37
  27.7 1.9 %copy.33.z_ref = f32[8,98,128]{2,1,0:T(8,128)} copy(f32[8,98,128]{2,0,1:T(8,128)} %bitcast.79) | data formatting | bytes 802816 | tf_op jit(solution)/shard_map/reshape | solution.py:536
  29.5 0.1 tile.49
  29.6 0.1 pad.19.clone
  29.7 0.3 fusion.11
  30.1 0.1 concatenate.26.coef
  30.2 0.1 fusion.20
  30.3 0.1 add_bitcast_fusion.2
  30.3 0.1 add_bitcast_fusion
  30.4 0.2 select_reduce_fusion.1
  30.6 0.1 fusion.2
  30.7 1.4 copy-done.1
  32.2 1.0 copy-done.3
  33.2 3.6 %shard_map.87 = (f32[8,98,128]{2,1,0:T(8,128)S(1)}, f32[8,98,128]{2,1,0:T(8,128)S(1)}, f32[40,128]{1,0:T(8,128)S(1)}) custom-call(s32[4,80]{1,0:T(4,128)S(1)} %pad_add_fusion.1.meta, s32[8]{0:T(128)S(1)} %broadcast_maximum_fusion.rep, f32[16,128]{1,0:T(8,128)S(1)} %concatenate.26.coef, f32[8,98,128]{2,1,0:T(8,128)S(1)} %copy-done.3, ...), custom_call_target="tpu_custom_call" | custom-call | flops 134217728 | bytes 8388608 | tf_op jit(solution)/shard_map/pallas_call | solution.py:328
  36.8 0.8 copy-done.8
  37.5 0.8 copy-done.10
  38.3 0.1 maximum_maximum_fusion.state
  38.4 0.1 compare_convert_fusion.same
  38.5 60.1 %all-to-all-done = bf16[4,8,400,128]{3,2,1,0:T(8,128)(2,1)S(1)} async-done(((bf16[4,8,400,128]{3,2,1,0:T(8,128)(2,1)}), bf16[4,8,400,128]{3,2,1,0:T(8,128)(2,1)S(1)}, u32[]{:S(2)}, u32[]{:S(2)}) %all-to-all-start) | async-done | bytes 3276832 | tf_op jit(solution)/shard_map/all_to_all | solution.py:500
  98.6 1.1 copy-done.4
  99.7 1.0 copy-done.9
  100.7 1.0 copy-done.11
  101.7 5.5 %shard_map.88 = (f32[8,98,128]{2,1,0:T(8,128)S(1)}, f32[8,98,128]{2,1,0:T(8,128)S(1)}, f32[40,128]{1,0:T(8,128)S(1)}) custom-call(s32[4,80]{1,0:T(4,128)S(1)} %pad_add_fusion.1.meta, s32[8]{0:T(128)S(1)} %broadcast_maximum_fusion.rep, f32[16,128]{1,0:T(8,128)S(1)} %concatenate.26.coef, f32[8,98,128]{2,1,0:T(8,128)S(1)} %copy-done.4, ...), custom_call_target="tpu_custom_call" | custom-call | flops 134217728 | bytes 8388608 | tf_op jit(solution)/shard_map/pallas_call | solution.py:328
  107.3 9.4 %shard_map.89 = (f32[16,128]{1,0:T(8,128)S(1)}, f32[16,128]{1,0:T(8,128)S(1)}) custom-call(f32[40,128]{1,0:T(8,128)S(1)} %get-tuple-element.29.mom.rest_3_, f32[16,128]{1,0:T(8,128)S(1)} %maximum_maximum_fusion.state, f32[128,128]{1,0:T(8,128)S(1)} %compare_convert_fusion.same), custom_call_target="tpu_custom_call" | custom-call | tf_op jit(solution)/shard_map/pallas_call | solution.py:447
  116.6 6.6 %shard_map.90 = (f32[8,98,128]{2,1,0:T(8,128)S(1)}, f32[40,128]{1,0:T(8,128)S(1)}) custom-call(s32[4,80]{1,0:T(4,128)S(1)} %pad_add_fusion.1.meta, s32[8]{0:T(128)S(1)} %broadcast_maximum_fusion.rep, f32[16,128]{1,0:T(8,128)S(1)} %get-tuple-element.30.coef, f32[8,98,128]{2,1,0:T(8,128)S(1)} %get-tuple-element.31.z_ref, ...), custom_call_target="tpu_custom_call" | custom-call | flops 134217728 | bytes 8388608 | tf_op jit(solution)/shard_map/pallas_call | solution.py:328
  123.3 8.8 %shard_map.91 = (f32[16,128]{1,0:T(8,128)S(1)}, f32[16,128]{1,0:T(8,128)S(1)}) custom-call(f32[40,128]{1,0:T(8,128)S(1)} %get-tuple-element.33.mom.rest_3_, f32[16,128]{1,0:T(8,128)S(1)} %get-tuple-element.34.state, f32[128,128]{1,0:T(8,128)S(1)} %compare_convert_fusion.same), custom_call_target="tpu_custom_call" | custom-call | tf_op jit(solution)/shard_map/pallas_call | solution.py:447
  132.1 0.0 copy-start.12
  132.1 6.6 %shard_map.92 = (f32[8,98,128]{2,1,0:T(8,128)S(1)}, f32[40,128]{1,0:T(8,128)S(1)}) custom-call(s32[4,80]{1,0:T(4,128)S(1)} %pad_add_fusion.1.meta, s32[8]{0:T(128)S(1)} %broadcast_maximum_fusion.rep, f32[16,128]{1,0:T(8,128)S(1)} %get-tuple-element.35.coef, f32[8,98,128]{2,1,0:T(8,128)S(1)} %get-tuple-element.36.z_ref, ...), custom_call_target="tpu_custom_call" | custom-call | flops 134217728 | bytes 8388608 | tf_op jit(solution)/shard_map/pallas_call | solution.py:328
  138.8 0.8 copy.38
  139.6 10.4 %shard_map.93 = (f32[16,128]{1,0:T(8,128)S(1)}, f32[16,128]{1,0:T(8,128)}) custom-call(f32[40,128]{1,0:T(8,128)S(1)} %get-tuple-element.38.mom, f32[16,128]{1,0:T(8,128)S(1)} %get-tuple-element.39.state, f32[128,128]{1,0:T(8,128)S(1)} %compare_convert_fusion.same), custom_call_target="tpu_custom_call" | custom-call | tf_op jit(solution)/shard_map/pallas_call | solution.py:447
  150.0 0.1 copy.34
  150.1 0.7 dynamic-slice_bitcast_fusion
  150.8 0.6 gather_fusion
  151.3 0.7 broadcast_select_fusion
  (45 shorter events, 0.3 us)
Async XLA Ops:
  12.2 1.7 %copy-start.6 = (bf16[16,2,3,12544]{3,1,2,0:T(2,128)(2,1)S(1)}, bf16[16,2,3,12544]{3,1,2,0:T(2,128)(2,1)}, u32[]{:S(2)}) copy-start(bf16[16,2,3,12544]{3,1,2,0:T(2,128)(2,1)} %param.7) | copy-start | bytes 7225348
  13.9 1.1 copy-start.7
  18.7 1.2 copy-start
  19.9 1.7 %copy-start.5 = (bf16[32,400,128]{2,1,0:T(8,128)(2,1)}, bf16[32,400,128]{2,1,0:T(8,128)(2,1)S(1)}, u32[]{:S(2)}) copy-start(bf16[32,400,128]{2,1,0:T(8,128)(2,1)S(1)} %get-tuple-element.24) | copy-start | bytes 9830404
  21.6 77.0 %all-to-all-start = ((bf16[4,8,400,128]{3,2,1,0:T(8,128)(2,1)}), bf16[4,8,400,128]{3,2,1,0:T(8,128)(2,1)S(1)}, u32[]{:S(2)}, u32[]{:S(2)}) async-start(bf16[4,8,400,128]{3,2,1,0:T(8,128)(2,1)} %bitcast.75), calls=%async_computation | async-start | bytes 6553600 | tf_op jit(solution)/shard_map/all_to_all | solution.py:500
  30.7 1.4 copy-start.1
  32.2 1.0 copy-start.3
  36.8 0.8 copy-start.8
  37.5 0.8 copy-start.10
  98.6 18.1 %copy-start.2 = (bf16[16,400,128]{2,1,0:T(8,128)(2,1)S(1)}, bf16[16,400,128]{2,1,0:T(8,128)(2,1)}, u32[]{:S(2)}) copy-start(bf16[16,400,128]{2,1,0:T(8,128)(2,1)} %copy-done) | copy-start | bytes 4915204
  98.6 1.1 copy-start.4
  99.7 1.0 copy-start.9
  100.7 1.0 copy-start.11
  132.1 19.2 %copy-start.12 = (f32[8,7]{1,0:T(8,128)S(1)}, f32[8,7]{1,0:T(8,128)}, u32[]{:S(2)}) copy-start(f32[8,7]{1,0:T(8,128)} %param.10) | copy-start | bytes 676
